TPU v7x, 256 devices: a whole 4x4x8 slice. The times are simulated.
256 devices in a mesh: grp: 16 (over x_hi, y, core), dev: 16 (over x_lo, z).
Axes of the slice: x: 4 (x_hi: 2, x_lo: 2; x = x_hi * 2 + x_lo), y: 4, z: 8, core: 2. Of those that a mesh axis runs over, the one named last changes fastest.
Arguments:
- series: bfloat16 [16384, 6, 1024], P(('grp', 'dev')), may hold values from -6 to 6
- taps: bfloat16 [16384, 64], P(('grp', 'dev')), may hold values from -0.75 to 0.75
- keep: int32 [16384, 6], P(('grp', 'dev')), may hold values from 0 to 1, as said below
- offsets: int32 [8], replicated, may hold values from 1 to 256, as said below
Outputs:
- corr: float32 [16384, 8, 128], P(('grp', 'dev'))
- stack: float32 [8, 128], replicated
Inputs may be any that keep to these rules, and one draw needn't show every extreme that they name: keep[c, s] is 1 where segment s of channel c is free of passing trains and usable; trains cover runs of neighbouring channels. 8 distinct channel offsets; 256 is always among them.
All inputs are finite; a program needn't handle non-finite values.
Results may differ from a plain program's by a relative error of at most 0.0041.
Values may be sent and summed in bfloat16 or wider, within the bound.
A program may use at most 128 MiB of HBM per device.

v0:
```python
import math

import jax
import jax.numpy as jnp
from jax import lax
from jax.sharding import PartitionSpec as P

SEG = 6
SAMP = 1024
BLK = 128
NLAG = 128
REACH = 256


def shifted(block, axis, distance):
    devices = range(lax.axis_size(axis))
    route = [((i - distance) % len(devices), i) for i in devices]
    return lax.ppermute(block, axis, route)


def toeplitz_rows(taps_part, block_len):
    row_total = taps_part.shape[0]
    tap_count = taps_part.shape[1]
    lead_zeros = jnp.zeros((row_total, block_len - tap_count + 1), taps_part.dtype)
    trail_zeros = jnp.zeros((row_total, block_len), taps_part.dtype)
    pattern = jnp.concatenate([lead_zeros, taps_part[:, ::-1], trail_zeros], axis=1)
    repeated = jnp.tile(pattern, (1, block_len))
    return repeated[:, : block_len * 2 * block_len].reshape(row_total, block_len, 2 * block_len)


def whiten_local(series_part, taps_part):
    row_total, segment_count, sample_count = series_part.shape
    blocks = series_part.reshape(row_total, segment_count, sample_count // BLK, BLK)
    earlier = jnp.concatenate([jnp.zeros_like(blocks[:, :, :1]), blocks[:, :, :-1]], axis=2)
    windows = jnp.concatenate([earlier, blocks], axis=3)
    matrix = toeplitz_rows(taps_part, BLK)
    filtered = jnp.einsum("csbi,cji->csbj", windows, matrix, preferred_element_type=jnp.float32)
    return filtered.reshape(row_total, segment_count, sample_count).astype(jnp.bfloat16)


def forward_table(input_len):
    transform_size = 2 * BLK
    sample_index = jnp.arange(input_len, dtype=jnp.int32)[:, None]
    cos_bins = jnp.arange(BLK + 1, dtype=jnp.int32)[None, :]
    sin_bins = jnp.arange(1, BLK, dtype=jnp.int32)[None, :]
    cos_phase = (sample_index * cos_bins % transform_size).astype(jnp.float32) * (
        2.0 * math.pi / transform_size
    )
    sin_phase = (sample_index * sin_bins % transform_size).astype(jnp.float32) * (
        2.0 * math.pi / transform_size
    )
    return jnp.concatenate([jnp.cos(cos_phase), -jnp.sin(sin_phase)], axis=1)


def split_table(table):
    high_part = lax.optimization_barrier(table.astype(jnp.bfloat16))
    low_part = (table - high_part.astype(jnp.float32)).astype(jnp.bfloat16)
    return (high_part, low_part)


def table_product(records, parts):
    return jnp.dot(records, parts[0], preferred_element_type=jnp.float32) + jnp.dot(
        records, parts[1], preferred_element_type=jnp.float32
    )


def lag_table():
    transform_size = 2 * BLK
    lag_index = jnp.arange(NLAG, dtype=jnp.int32)[None, :]
    cos_bins = jnp.arange(BLK + 1, dtype=jnp.int32)[:, None]
    sin_bins = jnp.arange(1, BLK, dtype=jnp.int32)[:, None]
    cos_weight = jnp.where((cos_bins == 0) | (cos_bins == BLK), 1.0, 2.0) / transform_size
    cos_phase = (cos_bins * lag_index % transform_size).astype(jnp.float32) * (
        2.0 * math.pi / transform_size
    )
    sin_phase = (sin_bins * lag_index % transform_size).astype(jnp.float32) * (
        2.0 * math.pi / transform_size
    )
    cos_part = jnp.cos(cos_phase) * cos_weight
    sin_part = jnp.sin(sin_phase) * (-2.0 / transform_size)
    return jnp.concatenate([cos_part, sin_part], axis=0)


def record_spectra(records, upper_parts, lower_parts):
    row_total = records.shape[0]
    half_lag = NLAG // 2
    padded = jnp.concatenate(
        [
            jnp.zeros((row_total, half_lag), jnp.bfloat16),
            records,
            jnp.zeros((row_total, BLK - half_lag), jnp.bfloat16),
        ],
        axis=1,
    )
    pieces = padded.reshape(row_total, SAMP // BLK + 1, BLK)
    first_half = table_product(pieces[:, :-1], upper_parts)
    return first_half + table_product(pieces[:, 1:], lower_parts)


def cross_spectra(own_spectra, partner_spectra):
    edge_bins = BLK + 1
    own_real = own_spectra[..., :edge_bins]
    own_imag = own_spectra[..., edge_bins:]
    far_real = partner_spectra[..., :edge_bins]
    far_imag = partner_spectra[..., edge_bins:]
    zero_column = jnp.zeros_like(own_imag[..., :1])
    own_imag_full = jnp.concatenate([zero_column, own_imag, zero_column], axis=-1)
    far_imag_full = jnp.concatenate([zero_column, far_imag, zero_column], axis=-1)
    real_part = jnp.sum(own_real * far_real + own_imag_full * far_imag_full, axis=-2)
    imag_part = jnp.sum(own_real[..., 1:BLK] * far_imag - own_imag * far_real[..., 1:BLK], axis=-2)
    return jnp.concatenate([real_part, imag_part], axis=-1)


def local(series, taps, keep, offsets):
    channels = series.shape[0]
    hop_count = REACH // channels
    offset_total = offsets.shape[0]
    keep_wire = keep.astype(jnp.bfloat16)
    own_white = whiten_local(series, taps)
    arrived = []
    for distance in range(1, hop_count + 1):
        arrived.append(shifted((own_white, keep_wire), ("grp", "dev"), -distance))
    partner_white = [received[0] for received in arrived]
    partner_keep = [received[1] for received in arrived]
    keep_own = keep.astype(jnp.float32)
    keep_near = jnp.concatenate([keep_wire] + partner_keep, axis=0).astype(jnp.float32)
    partner_rows = offsets[:, None] + jnp.arange(channels, dtype=jnp.int32)[None, :]
    paired = keep_own[None, :, :] * keep_near[partner_rows]
    pair_count = jnp.sum(paired, axis=2)
    block_parts = split_table(forward_table(BLK))
    window_table = forward_table(2 * BLK)
    upper_parts = split_table(window_table[:BLK])
    lower_parts = split_table(window_table[BLK:])
    accumulated = jnp.zeros((offset_total, channels, 2 * BLK), jnp.float32)
    for segment in range(SEG):
        weights = paired[:, :, segment]
        nearby = jnp.concatenate(
            [own_white[:, segment]] + [white[:, segment] for white in partner_white], axis=0
        )
        near_spectra = record_spectra(nearby, upper_parts, lower_parts)
        own_blocks = own_white[:, segment].reshape(channels, SAMP // BLK, BLK)
        own_spectra = table_product(own_blocks, block_parts)

        def offset_terms(offset_value):
            partner = lax.dynamic_slice_in_dim(near_spectra, offset_value, channels, 0)
            return cross_spectra(own_spectra, partner)

        spectra_terms = lax.map(offset_terms, offsets)
        accumulated = accumulated + weights[:, :, None] * spectra_terms
    lag_values = jnp.dot(accumulated, lag_table(), precision=lax.Precision.HIGHEST)
    divisor = jnp.maximum(pair_count, 1.0)[:, :, None] * math.sqrt(SAMP)
    corr = jnp.transpose(lag_values / divisor, (1, 0, 2))
    partial_sum = jnp.sum(corr, axis=0)
    stack = lax.psum(partial_sum, ("grp", "dev")) / math.sqrt(
        channels * lax.axis_size(("grp", "dev"))
    )
    return (corr, stack)


def solution(mesh):
    in_specs = (
        P(("grp", "dev"), None, None),
        P(("grp", "dev"), None),
        P(("grp", "dev"), None),
        P(),
    )
    out_specs = (P(("grp", "dev"), None, None), P())
    return jax.shard_map(local, mesh=mesh, in_specs=in_specs, out_specs=out_specs, check_vma=False)
```

profile of v0, /device:TPU:1, one launch (start us, length us, event | category | flops | bytes accessed | tf_op | source)
XLA Modules:
  0.0 685.6 jit_solution(6252859585116331420)
XLA Ops:
  1.4 7.9 %collective-permute-start = (bf16[64,6]{0,1:T(8,128)(2,1)S(1)}, bf16[64,6]{0,1:T(8,128)(2,1)S(1)}, u32[]{:S(2)}, u32[]{:S(2)}) collective-permute-start(bf16[64,6]{0,1:T(8,128)(2,1)S(1)} %get-tuple-element.315), channel_id=1, source_target_pairs={{1,0},{2,1},{3,2},{4,3},{5,4},{6,5},{7,6},{8,7},{9,8},{10,9},{11,1... | collective-permute-start | bytes 2312 | tf_op jit(solution)/shard_map/ppermute | solution.py:18
  11.2 5.0 collective-permute-start.3
  18.0 3.2 tile.4
  21.2 10.9 %tile.10 = bf16[64,32896]{1,0:T(8,128)(2,1)} reshape(bf16[64,128,257]{2,1,0:T(8,128)(2,1)} %tile.4) | data formatting | bytes 8421376 | tf_op jit(solution)/shard_map/tile | solution.py:27
  54.0 9.1 %collective-permute-start.7 = (bf16[64,6,1024]{2,0,1:T(8,128)(2,1)}, bf16[64,6,1024]{2,0,1:T(8,128)(2,1)}, u32[]{:S(2)}, u32[]{:S(2)}) collective-permute-start(bf16[64,6,1024]{2,0,1:T(8,128)(2,1)} %convert_element_type.64), channel_id=1, source_target_pairs={{4,0},{5,1},{6,2},{7,3},{8,4},{9,5},{10,6},{11,7},{12,8},{13,9},{1... | collective-permute-start | bytes 2359304 | tf_op jit(solution)/shard_map/ppermute | solution.py:18
  68.3 21.4 %collective-permute-done.5 = bf16[64,6,1024]{2,0,1:T(8,128)(2,1)} collective-permute-done((bf16[64,6,1024]{2,0,1:T(8,128)(2,1)}, bf16[64,6,1024]{2,0,1:T(8,128)(2,1)}, u32[]{:S(2)}, u32[]{:S(2)}) %collective-permute-start.5) | collective-permute-done | bytes 786464 | tf_op jit(solution)/shard_map/ppermute | solution.py:18
  91.8 39.8 %collective-permute-done.6 = bf16[64,6,1024]{2,0,1:T(8,128)(2,1)} collective-permute-done((bf16[64,6,1024]{2,0,1:T(8,128)(2,1)}, bf16[64,6,1024]{2,0,1:T(8,128)(2,1)}, u32[]{:S(2)}, u32[]{:S(2)}) %collective-permute-start.6) | collective-permute-done | bytes 786464 | tf_op jit(solution)/shard_map/ppermute | solution.py:18
  160.3 3.2 fusion.198
  175.3 3.1 fusion.199
  190.1 3.2 fusion.200
  220.0 3.1 fusion.202
  229.6 3.9 add_add_fusion.5
  234.4 48.4 %while.60 = (s32[]{:T(128)}, f32[8,64,256]{2,1,0:T(8,128)}, f32[64,8,256]{2,1,0:T(8,128)S(1)}, s32[8]{0:T(128)S(1)}, f32[320,8,256]{2,1,0:T(8,128)}, /*index=5*/...) while((s32[]{:T(128)}, f32[8,64,256]{2,1,0:T(8,128)}, f32[64,8,256]{2,1,0:T(8,128)S(1)}, ...), condition=%wide.region_3.4_spmd, body=%wide.region_0.3_spmd.sunk | while | flops 788487 | bytes 2810567 | solution.py:148
  286.2 4.0 add_add_fusion.4
  290.2 43.5 %while.61 = (s32[]{:T(128)}, f32[8,64,256]{2,1,0:T(8,128)S(1)}, f32[64,8,256]{2,1,0:T(8,128)S(1)}, s32[8]{0:T(128)S(1)}, f32[320,8,256]{2,1,0:T(8,128)}, /*index...) while((s32[]{:T(128)}, f32[8,64,256]{2,1,0:T(8,128)S(1)}, ...), condition=%wide.region_7.8_spmd, body=%wide.region_4.7_spmd.sunk | while | flops 788487 | bytes 2842827 | solution.py:148
  337.8 3.9 add_add_fusion.3
  341.7 43.5 %while.62 = (s32[]{:T(128)}, f32[8,64,256]{2,1,0:T(8,128)S(1)}, f32[64,8,256]{2,1,0:T(8,128)S(1)}, s32[8]{0:T(128)S(1)}, f32[320,8,256]{2,1,0:T(8,128)}, /*index...) while((s32[]{:T(128)}, f32[8,64,256]{2,1,0:T(8,128)S(1)}, ...), condition=%wide.region_11.12_spmd, body=%wide.region_8.11_spmd.sunk | while | flops 788487 | bytes 2842827 | solution.py:148
  389.3 3.9 add_add_fusion.2
  394.0 48.4 %while.63 = (s32[]{:T(128)}, f32[8,64,256]{2,1,0:T(8,128)}, f32[64,8,256]{2,1,0:T(8,128)S(1)}, s32[8]{0:T(128)S(1)}, f32[320,8,256]{2,1,0:T(8,128)}, /*index=5*/...) while((s32[]{:T(128)}, f32[8,64,256]{2,1,0:T(8,128)}, f32[64,8,256]{2,1,0:T(8,128)S(1)}, ...), condition=%wide.region_15.16_spmd, body=%wide.region_12.15_spmd.sunk | while | flops 788487 | bytes 2810567 | solution.py:148
  444.7 4.0 add_add_fusion.1
  449.6 48.6 %while.64 = (s32[]{:T(128)}, f32[8,64,256]{2,1,0:T(8,128)}, f32[64,8,256]{2,1,0:T(8,128)S(1)}, s32[8]{0:T(128)S(1)}, f32[320,8,256]{2,1,0:T(8,128)}, /*index=5*/...) while((s32[]{:T(128)}, f32[8,64,256]{2,1,0:T(8,128)}, f32[64,8,256]{2,1,0:T(8,128)S(1)}, ...), condition=%wide.region_19.20_spmd, body=%wide.region_16.19_spmd.sunk | while | flops 788487 | bytes 2810567 | solution.py:148
  500.4 4.0 add_add_fusion
  504.5 43.5 %while.65 = (s32[]{:T(128)}, f32[8,64,256]{2,1,0:T(8,128)S(1)}, f32[64,8,256]{2,1,0:T(8,128)S(1)}, s32[8]{0:T(128)S(1)}, f32[320,8,256]{2,1,0:T(8,128)}, /*index...) while((s32[]{:T(128)}, f32[8,64,256]{2,1,0:T(8,128)S(1)}, ...), condition=%wide.region_23.24_spmd, body=%wide.region_20.23_spmd.sunk | while | flops 788487 | bytes 2842827 | solution.py:148
  551.1 133.6 %psum.7 = f32[8,128]{1,0:T(8,128)S(1)} all-reduce(f32[8,128]{1,0:T(8,128)S(1)} %get-tuple-element.316), channel_id=1, replica_groups=mesh['grp'=16,'dev'=16] {'grp','dev'}, use_global_device_ids=true, to_apply=%region_26.27 | all-reduce | flops 1024 | bytes 8192 | tf_op jit(solution)/shard_map/psum | solution.py:154
  (418 shorter events, 322.4 us)
Async XLA Ops:
  0.6 17.0 %copy-start.24 = (bf16[64,64]{1,0:T(8,128)(2,1)S(1)}, bf16[64,64]{1,0:T(8,128)(2,1)}, u32[]{:S(2)}) copy-start(bf16[64,64]{1,0:T(8,128)(2,1)} %param.17) | copy-start | bytes 24580
  1.4 51.0 %collective-permute-start = (bf16[64,6]{0,1:T(8,128)(2,1)S(1)}, bf16[64,6]{0,1:T(8,128)(2,1)S(1)}, u32[]{:S(2)}, u32[]{:S(2)}) collective-permute-start(bf16[64,6]{0,1:T(8,128)(2,1)S(1)} %get-tuple-element.315), channel_id=1, source_target_pairs={{1,0},{2,1},{3,2},{4,3},{5,4},{6,5},{7,6},{8,7},{9,8},{10,9},{11,1... | collective-permute-start | bytes 2312 | tf_op jit(solution)/shard_map/ppermute | solution.py:18
  9.3 43.8 %collective-permute-start.1 = (bf16[64,6]{0,1:T(8,128)(2,1)S(1)}, bf16[64,6]{0,1:T(8,128)(2,1)S(1)}, u32[]{:S(2)}, u32[]{:S(2)}) collective-permute-start(bf16[64,6]{0,1:T(8,128)(2,1)S(1)} %get-tuple-element.315), channel_id=1, source_target_pairs={{2,0},{3,1},{4,2},{5,3},{6,4},{7,5},{8,6},{9,7},{10,8},{11,9},{12,... | collective-permute-start | bytes 2312 | tf_op jit(solution)/shard_map/ppermute | solution.py:18
  10.8 43.3 %collective-permute-start.2 = (bf16[64,6]{0,1:T(8,128)(2,1)S(1)}, bf16[64,6]{0,1:T(8,128)(2,1)S(1)}, u32[]{:S(2)}, u32[]{:S(2)}) collective-permute-start(bf16[64,6]{0,1:T(8,128)(2,1)S(1)} %get-tuple-element.315), channel_id=1, source_target_pairs={{3,0},{4,1},{5,2},{6,3},{7,4},{8,5},{9,6},{10,7},{11,8},{12,9},{13... | collective-permute-start | bytes 2312 | tf_op jit(solution)/shard_map/ppermute | solution.py:18
  11.2 51.9 %collective-permute-start.3 = (bf16[64,6]{0,1:T(8,128)(2,1)S(1)}, bf16[64,6]{0,1:T(8,128)(2,1)S(1)}, u32[]{:S(2)}, u32[]{:S(2)}) collective-permute-start(bf16[64,6]{0,1:T(8,128)(2,1)S(1)} %get-tuple-element.315), channel_id=1, source_target_pairs={{4,0},{5,1},{6,2},{7,3},{8,4},{9,5},{10,6},{11,7},{12,8},{13,9},{1... | collective-permute-start | bytes 2312 | tf_op jit(solution)/shard_map/ppermute | solution.py:18
  32.0 2.2 slice-start
  38.3 27.8 %collective-permute-start.4 = (bf16[64,6,1024]{2,0,1:T(8,128)(2,1)}, bf16[64,6,1024]{2,0,1:T(8,128)(2,1)}, u32[]{:S(2)}, u32[]{:S(2)}) collective-permute-start(bf16[64,6,1024]{2,0,1:T(8,128)(2,1)} %convert_element_type.64), channel_id=1, source_target_pairs={{1,0},{2,1},{3,2},{4,3},{5,4},{6,5},{7,6},{8,7},{9,8},{10,9},{11,1... | collective-permute-start | bytes 2359304 | tf_op jit(solution)/shard_map/ppermute | solution.py:18
  42.9 4.6 copy-start.16
  52.4 37.2 %collective-permute-start.5 = (bf16[64,6,1024]{2,0,1:T(8,128)(2,1)}, bf16[64,6,1024]{2,0,1:T(8,128)(2,1)}, u32[]{:S(2)}, u32[]{:S(2)}) collective-permute-start(bf16[64,6,1024]{2,0,1:T(8,128)(2,1)} %convert_element_type.64), channel_id=1, source_target_pairs={{2,0},{3,1},{4,2},{5,3},{6,4},{7,5},{8,6},{9,7},{10,8},{11,9},{12,... | collective-permute-start | bytes 2359304 | tf_op jit(solution)/shard_map/ppermute | solution.py:18
  53.1 78.5 %collective-permute-start.6 = (bf16[64,6,1024]{2,0,1:T(8,128)(2,1)}, bf16[64,6,1024]{2,0,1:T(8,128)(2,1)}, u32[]{:S(2)}, u32[]{:S(2)}) collective-permute-start(bf16[64,6,1024]{2,0,1:T(8,128)(2,1)} %convert_element_type.64), channel_id=1, source_target_pairs={{3,0},{4,1},{5,2},{6,3},{7,4},{8,5},{9,6},{10,7},{11,8},{12,9},{13... | collective-permute-start | bytes 2359304 | tf_op jit(solution)/shard_map/ppermute | solution.py:18
  54.0 79.7 %collective-permute-start.7 = (bf16[64,6,1024]{2,0,1:T(8,128)(2,1)}, bf16[64,6,1024]{2,0,1:T(8,128)(2,1)}, u32[]{:S(2)}, u32[]{:S(2)}) collective-permute-start(bf16[64,6,1024]{2,0,1:T(8,128)(2,1)} %convert_element_type.64), channel_id=1, source_target_pairs={{4,0},{5,1},{6,2},{7,3},{8,4},{9,5},{10,6},{11,7},{12,8},{13,9},{1... | collective-permute-start | bytes 2359304 | tf_op jit(solution)/shard_map/ppermute | solution.py:18
  143.1 5.5 copy-start.13
  145.5 3.1 copy-start.7
  160.3 3.2 copy-start.8
  175.3 3.1 copy-start.9
  190.1 3.2 copy-start.10
  205.0 3.1 copy-start.11
  220.0 3.1 copy-start.6
  394.0 48.4 %copy-start.15 = (bf16[320,8,128]{0,2,1:T(8,128)(2,1)S(1)}, bf16[320,8,128]{0,2,1:T(8,128)(2,1)}, u32[]{:S(2)}) copy-start(bf16[320,8,128]{0,2,1:T(8,128)(2,1)} %get-tuple-element.265) | copy-start | bytes 1966084
  449.6 48.7 %copy-start.14 = (bf16[320,8,128]{0,2,1:T(8,128)(2,1)S(1)}, bf16[320,8,128]{0,2,1:T(8,128)(2,1)}, u32[]{:S(2)}) copy-start(bf16[320,8,128]{0,2,1:T(8,128)(2,1)} %get-tuple-element.267) | copy-start | bytes 1966084
  504.5 43.5 %copy-start.18 = (f32[8,64,256]{2,1,0:T(8,128)S(1)}, f32[8,64,256]{2,1,0:T(8,128)}, u32[]{:S(2)}) copy-start(f32[8,64,256]{2,1,0:T(8,128)} %copy-done.17) | copy-start | bytes 1572868
  504.5 43.5 %copy-start.20 = (f32[8,64,256]{2,1,0:T(8,128)S(1)}, f32[8,64,256]{2,1,0:T(8,128)}, u32[]{:S(2)}) copy-start(f32[8,64,256]{2,1,0:T(8,128)} %copy-done.19) | copy-start | bytes 1572868
  504.5 43.5 %copy-start.22 = (f32[129,128]{1,0:T(8,128)S(1)}, f32[129,128]{1,0:T(8,128)}, u32[]{:S(2)}) copy-start(f32[129,128]{1,0:T(8,128)} %fusion.122) | copy-start | bytes 198148
  504.5 43.5 %copy-start.23 = (f32[127,128]{1,0:T(8,128)S(1)}, f32[127,128]{1,0:T(8,128)}, u32[]{:S(2)}) copy-start(f32[127,128]{1,0:T(8,128)} %fusion.135) | copy-start | bytes 195076
  (11 other events, 17.5 us)
where the time goes:
time: 698 us; the launch traced here: 686 us
  other arithmetic  160 us (23%)
  local copies, waits for them, and re-layouts  143 us (20%)
  blocking collectives  134 us (19%)
  loops' own time  94.5 us (14%)
  matrix products  65.1 us (9%)
  waiting for transfers between devices  61.2 us (9%)
  starting transfers between devices  27 us (4%)
    psum x1, blocking collectives, local(): lax.psum(partial_sum, ('grp', 'dev'))  134 us
    another operation x6, loops' own time, local(): spectra_terms = lax.map(offset_terms, offsets)  94.5 us
    reduce_sum x48, other arithmetic, cross_spectra(): jnp.sum(own_real * far_real + own_imag_full * far_imag_full, axis=-2)  67.2 us
    reduce_sum x48, other arithmetic, cross_spectra(): jnp.sum(own_real[..., 1:BLK] * far_imag - own_imag * far_real[..., 1:BLK]...  66.3 us
    ppermute x8, waiting for transfers between devices, shifted(): return lax.ppermute(block, axis, route)  61.2 us
    unnamed x78, local copies, waits for them, and re-layouts  44 us
    dot_general x18, matrix products, table_product(): jnp.dot(records, parts[1], preferred_element_type=jnp.float32)  42.8 us
    dynamic_slice x48, local copies, waits for them, and re-layouts, local(): spectra_terms = lax.map(offset_terms, offsets)  28 us
  transfers between devices with their start and end apart: 8, of which 2 were waited for; matrix products, arithmetic and copies ran while one was open for 6% of the time, Pallas kernels for 0%

commit v1 on v0

v1 whole, which is shorter than its diff:
```python
import functools
import math

import jax
import jax.numpy as jnp
import numpy as np
from jax import lax
from jax.experimental import pallas as pl
from jax.experimental.pallas import tpu as pltpu
from jax.sharding import PartitionSpec as P

SEG = 6
SAMP = 1024
BLK = 128
NLAG = 128
NOFF = 8
CH = 64
NB = SAMP // BLK
NEAR = 3 * CH
GRP_CH = 16
MESH = pl.DeviceIdType.MESH


def dft_tables():
    n = np.arange(2 * BLK, dtype=np.float64)[:, None]
    f = np.arange(BLK, dtype=np.float64)[None, :] + 0.5
    ang = 2.0 * np.pi * f * n / (2 * BLK)
    full = np.concatenate([np.cos(ang), -np.sin(ang)], axis=1)
    half = BLK // 2
    own = full[:BLK]
    win = np.concatenate([full[half : half + BLK], full[half + BLK :], full[:half]], axis=0)

    def split(t):
        t32 = t.astype(np.float32)
        hi = t32.astype(jnp.bfloat16)
        lo = (t32 - hi.astype(np.float32)).astype(jnp.bfloat16)
        return hi, lo

    own_hi, own_lo = split(own)
    win_hi, win_lo = split(win)
    m = np.arange(NLAG, dtype=np.float64)[None, :]
    ang_inv = 2.0 * np.pi * f.T * m / (2 * BLK)
    inv = np.concatenate([np.cos(ang_inv), -np.sin(ang_inv)], axis=0) / BLK
    return (
        np.concatenate([own_hi, own_lo], axis=0),
        win_hi,
        win_lo,
        inv.astype(np.float32),
    )


def kernel(
    shape,
    ser,
    taps,
    keepv,
    keeps,
    offs,
    offv,
    t_own,
    t_hi,
    t_lo,
    t_inv,
    out,
    part,
    white,
    p1,
    p2,
    m2,
    k1,
    k2,
    km2,
    scr,
    keep_left,
    keep_near,
    xs,
    ys,
    accr,
    acci,
    cnt,
    res,
    res_send,
    res_recv,
    ssem,
    rsem,
):
    ng, nd = shape

    def dev(k):
        t = lax.axis_index("grp") * nd + lax.axis_index("dev") + (k + ng * nd)
        t = lax.rem(t, ng * nd)
        return (t // nd, lax.rem(t, nd))

    bar = pltpu.get_barrier_semaphore()
    for k in (-2, -1, 1, 2):
        pl.semaphore_signal(bar, inc=1, device_id=dev(k), device_id_type=MESH)

    for s in range(SEG):
        scr[pl.ds(s * 9 * GRP_CH, GRP_CH), :] = jnp.zeros((GRP_CH, BLK), jnp.float32)
    ri = lax.broadcasted_iota(jnp.int32, (BLK, BLK), 0)
    ci = lax.broadcasted_iota(jnp.int32, (BLK, BLK), 1)
    causal = ci >= ri

    @pl.loop(0, CH // GRP_CH)
    def _(g):
        for s in range(SEG):
            x = ser[s, pl.ds(g * GRP_CH, GRP_CH), :].astype(jnp.float32)
            for b in range(NB):
                scr[pl.ds((s * 9 + b + 1) * GRP_CH, GRP_CH), :] = x[:, b * BLK : (b + 1) * BLK]

        @pl.loop(0, GRP_CH // 2)
        def _(h):
            rows = []
            for e in range(2):
                c = h * 2 + e
                cur = [scr[pl.ds((s * 9 + 1) * GRP_CH + c, NB, stride=GRP_CH), :] for s in range(SEG)]
                prv = [scr[pl.ds(s * 9 * GRP_CH + c, NB, stride=GRP_CH), :] for s in range(SEG)]
                x = jnp.concatenate(
                    [jnp.concatenate(prv, axis=0), jnp.concatenate(cur, axis=0)], axis=1
                ).astype(jnp.bfloat16)
                row = taps[pl.ds(g * GRP_CH + c, 1), :]
                circ = pltpu.roll(jnp.broadcast_to(row, (BLK, BLK)), 0, 1, stride=1, stride_axis=0)
                toep = jnp.concatenate(
                    [jnp.where(causal, 0.0, circ), jnp.where(causal, circ, 0.0)], axis=0
                ).astype(jnp.bfloat16)
                rows.append(jnp.dot(x, toep, preferred_element_type=jnp.float32))
            for s in range(SEG):
                both = []
                for e in range(2):
                    flag = keeps[s, g * GRP_CH + h * 2 + e].astype(jnp.float32)
                    both.append(rows[e][s * NB : (s + 1) * NB] * flag)
                at = pl.multiple_of((g * GRP_CH + h * 2) * NB, 2 * NB)
                white[s, pl.ds(at, 2 * NB), :] = jnp.concatenate(both, axis=0).astype(jnp.bfloat16)

    pl.semaphore_wait(bar, 4)

    def remote(src, dst, lane, at, to):
        return pltpu.make_async_remote_copy(
            src_ref=src,
            dst_ref=dst,
            send_sem=ssem.at[lane, at],
            recv_sem=rsem.at[lane, at],
            device_id=dev(to),
            device_id_type=MESH,
        )

    def keep_copy(lane):
        if lane == 0:
            return remote(keepv, k1, 0, SEG, -1)
        if lane == 1:
            return remote(k1, k2, 1, SEG, -1)
        return remote(keepv, km2, 2, SEG, 2)

    def seg_copy(lane, s):
        if lane == 0:
            return remote(white.at[s], p1.at[s], 0, s, -1)
        if lane == 1:
            return remote(p1.at[s], p2.at[s], 1, s, -1)
        return remote(white.at[s], m2.at[s], 2, s, 2)

    keep_copy(0).start()
    keep_copy(2).start()

    @pl.loop(0, SEG)
    def _(s):
        seg_copy(0, s).start()
        seg_copy(2, s).start()

    keep_copy(0).wait_recv()
    keep_copy(1).start()

    zero = jnp.zeros((64, BLK), jnp.float32)

    @pl.loop(0, CH * NOFF * 8 // 64)
    def _(i):
        accr[pl.ds(i * 64, 64), :] = zero
        acci[pl.ds(i * 64, 64), :] = zero

    keep_left[pl.ds(0, CH), :] = keepv[...].astype(jnp.float32)
    keep_near[pl.ds(0, CH), :] = keepv[...].astype(jnp.float32)
    keep_near[pl.ds(CH, CH), :] = k1[...].astype(jnp.float32)

    def pair_rows(r, j):
        row = r + offs[j]
        home = row < NEAR
        return jnp.where(home, r, CH + r), jnp.where(home, row, row - 2 * CH)

    lane_i = lax.broadcasted_iota(jnp.int32, (16, NB, BLK), 2)
    blk_i = lax.broadcasted_iota(jnp.int32, (16, NB, BLK), 1)
    low = lane_i < BLK // 2
    first = blk_i == 0
    last = blk_i == NB - 1

    def window_dft(src, s, base):
        @pl.loop(0, CH // 16)
        def _(i):
            w = src[s, pl.ds(i * 128, 128), :]
            wf = w.astype(jnp.float32).reshape(16, NB, BLK)
            nxt = jnp.where(last, 0.0, pltpu.roll(wf, NB - 1, 1))
            prv = jnp.where(first, 0.0, pltpu.roll(wf, 1, 1))
            mix = jnp.where(low, nxt, prv).reshape(128, BLK).astype(jnp.bfloat16)
            x = jnp.concatenate([w, mix], axis=1)
            y = jnp.dot(x, t_hi[...], preferred_element_type=jnp.float32)
            y = y + jnp.dot(x, t_lo[...], preferred_element_type=jnp.float32)
            ys[pl.ds(base + i * 16, 16), :, :] = y.reshape(16, NB, 2 * BLK)

    def own_dft(src, s, base):
        @pl.loop(0, CH // 16)
        def _(i):
            w = src[s, pl.ds(i * 128, 128), :]
            x = jnp.concatenate([w, w], axis=1)
            y = jnp.dot(x, t_own[...], preferred_element_type=jnp.float32)
            xs[pl.ds(base + i * 16, 16), :, :] = y.reshape(16, NB, 2 * BLK)

    @pl.loop(0, SEG)
    def _(s):
        own_dft(white, s, 0)
        window_dft(white, s, 0)
        seg_copy(0, s).wait_recv()
        seg_copy(1, s).start()
        window_dft(p1, s, CH)
        seg_copy(2, s).wait_recv()
        own_dft(m2, s, CH)
        seg_copy(1, s).wait_recv()
        window_dft(p2, s, 2 * CH)

        @pl.loop(0, CH)
        def _(r):
            for j in range(NOFF):
                left, near = pair_rows(r, j)
                a = xs[left]
                b = ys[near]
                at = pl.ds(pl.multiple_of((r * NOFF + j) * 8, 8), 8)
                ar, ai = a[:, :BLK], a[:, BLK:]
                br, bi = b[:, :BLK], b[:, BLK:]
                accr[at, :] += ar * br + ai * bi
                acci[at, :] += ar * bi - ai * br

    keep_copy(1).wait_recv()
    keep_copy(2).wait_recv()
    keep_near[pl.ds(2 * CH, CH), :] = k2[...].astype(jnp.float32)
    keep_left[pl.ds(CH, CH), :] = km2[...].astype(jnp.float32)

    @pl.loop(0, CH)
    def _(r):
        prod = []
        for j in range(NOFF):
            left, near = pair_rows(r, j)
            prod.append(keep_left[pl.ds(left, 1), :] * keep_near[pl.ds(near, 1), :])
        at = pl.ds(pl.multiple_of(r * NOFF, NOFF), NOFF)
        cnt[at, :] = jnp.concatenate(prod, axis=0)

    ones = jnp.ones((BLK, BLK), jnp.bfloat16)
    part[...] = jnp.zeros((NOFF, NLAG), jnp.float32)

    def back_copy(q):
        rows = pl.ds(q * 128, 128)
        return remote(res_send.at[rows], res_recv.at[rows], 3, q, -2)

    for q in range(4):
        base = q * 128
        sr = jnp.zeros((128, BLK), jnp.float32)
        si = jnp.zeros((128, BLK), jnp.float32)
        for k in range(8):
            sr = sr + accr[pl.ds(base * 8 + k, 128, stride=8), :]
            si = si + acci[pl.ds(base * 8 + k, 128, stride=8), :]
        spec = jnp.concatenate([sr, si], axis=1)
        lag = jnp.dot(
            spec, t_inv[...], precision=lax.Precision.HIGHEST, preferred_element_type=jnp.float32
        )
        number = jnp.dot(
            cnt[pl.ds(base, 128), :].astype(jnp.bfloat16), ones, preferred_element_type=jnp.float32
        )
        corr = lag / (jnp.maximum(number, 1.0) * math.sqrt(SAMP))
        res[pl.ds(base, 128), :] = corr
        res_send[pl.ds(base, 128), :] = corr.astype(res_send.dtype)
        back_copy(q).start()
        part[...] += jnp.sum(corr.reshape(16, NOFF, NLAG), axis=0)

    for q in range(4):
        back_copy(q).wait_recv()
        for i in range(16):
            r = q * 16 + i
            home = offv[...] + r < NEAR
            got = res_recv[pl.ds(q * 128, 128), :].astype(jnp.float32)[i * 8 : (i + 1) * 8]
            out[r] = jnp.where(home, res[pl.ds(r * 8, 8), :], got)

    for q in range(4):
        back_copy(q).wait_send()

    @pl.loop(0, SEG)
    def _(s):
        for lane in range(3):
            seg_copy(lane, s).wait_send()

    for lane in range(3):
        keep_copy(lane).wait_send()


def local(shape, series, taps, keep, offsets):
    t_own, t_hi, t_lo, t_inv = dft_tables()
    ser = jnp.transpose(series, (1, 0, 2))
    taps_row = jnp.pad(taps.astype(jnp.float32), ((0, 0), (0, BLK - taps.shape[1])))
    keepv = jnp.pad(keep.astype(jnp.bfloat16), ((0, 0), (0, BLK - SEG)))
    keeps = jnp.transpose(keep, (1, 0))
    offv = jnp.broadcast_to(offsets[:, None], (NOFF, NLAG))
    vmem = pl.BlockSpec(memory_space=pltpu.VMEM)
    smem = pl.BlockSpec(memory_space=pltpu.SMEM)
    f32, b16 = jnp.float32, jnp.bfloat16
    rows = CH * NB
    corr, part = pl.pallas_call(
        functools.partial(kernel, shape),
        out_shape=(
            jax.ShapeDtypeStruct((CH, NOFF, NLAG), f32),
            jax.ShapeDtypeStruct((NOFF, NLAG), f32),
        ),
        in_specs=[vmem, vmem, vmem, smem, smem, vmem, vmem, vmem, vmem, vmem],
        out_specs=(vmem, vmem),
        scratch_shapes=[
            pltpu.VMEM((SEG, rows, BLK), b16),
            pltpu.VMEM((SEG, rows, BLK), b16),
            pltpu.VMEM((SEG, rows, BLK), b16),
            pltpu.VMEM((SEG, rows, BLK), b16),
            pltpu.VMEM((CH, BLK), b16),
            pltpu.VMEM((CH, BLK), b16),
            pltpu.VMEM((CH, BLK), b16),
            pltpu.VMEM((SEG * 9 * GRP_CH, BLK), f32),
            pltpu.VMEM((2 * CH, BLK), f32),
            pltpu.VMEM((NEAR, BLK), f32),
            pltpu.VMEM((2 * CH, NB, 2 * BLK), f32),
            pltpu.VMEM((NEAR, NB, 2 * BLK), f32),
            pltpu.VMEM((CH * NOFF * 8, BLK), f32),
            pltpu.VMEM((CH * NOFF * 8, BLK), f32),
            pltpu.VMEM((CH * NOFF, BLK), f32),
            pltpu.VMEM((CH * NOFF, BLK), f32),
            pltpu.VMEM((CH * NOFF, BLK), b16),
            pltpu.VMEM((CH * NOFF, BLK), b16),
            pltpu.SemaphoreType.DMA((4, SEG + 1)),
            pltpu.SemaphoreType.DMA((4, SEG + 1)),
        ],
        compiler_params=pltpu.CompilerParams(
            collective_id=0, has_side_effects=True, vmem_limit_bytes=40 << 20
        ),
        name="whiten_correlate",
    )(ser, taps_row, keepv, keeps, offsets, offv, t_own, t_hi, t_lo, t_inv)
    stack = lax.psum(part, ("grp", "dev")) / math.sqrt(CH * shape[0] * shape[1])
    return corr, stack


def solution(mesh):
    spec3 = P(("grp", "dev"), None, None)
    spec2 = P(("grp", "dev"), None)
    shape = (mesh.shape["grp"], mesh.shape["dev"])
    return jax.shard_map(
        functools.partial(local, shape),
        mesh=mesh,
        in_specs=(spec3, spec2, spec2, P()),
        out_specs=(spec3, P()),
        check_vma=False,
    )
```

time: 698 us -> 175 us (0.25); the launches traced: 686 us -> 175 us
  other arithmetic: 160 us -> 1.3 us
  local copies, waits for them, and re-layouts: 143 us -> 7.02 us
  loops' own time: 94.5 us -> 0 us
  Pallas kernels: 0 us -> 81 us
  matrix products: 65.1 us -> 0 us
  waiting for transfers between devices: 61.2 us -> 0 us
  blocking collectives: 134 us -> 84.7 us
  starting transfers between devices: 27 us -> 0 us
    reduce_sum x97 -> x0, other arithmetic: 134 us -> none  [the longest x48 67.2 us: cross_spectra(): jnp.sum(own_real * far_real + own_imag_full * far_imag_full, axis=-2)]
    another operation x6 -> x0, loops' own time: 94.5 us -> none  [local(): spectra_terms = lax.map(offset_terms, offsets)]
    pallas_call x0 -> x1, Pallas kernels: none -> 81 us  [local(): pl.pallas_call(functools.partial(kernel, shape), out_shape=(jax.ShapeDtyp...]
    dot_general x38 -> x0, matrix products: 65.1 us -> none  [the longest x18 42.8 us: table_product(): jnp.dot(records, parts[1], preferred_element_type=jnp.float32)]
    ppermute x8 -> x0, waiting for transfers between devices: 61.2 us -> none  [shifted(): return lax.ppermute(block, axis, route)]
    psum x1, blocking collectives: 134 us -> 84.7 us  [local(): stack = lax.psum(part, ('grp', 'dev')) / math.sqrt(CH * shape[0] * shape[1])]
    unnamed x78 -> x17, local copies, waits for them, and re-layouts: 44 us -> 6.83 us
    concatenate x16 -> x0, local copies, waits for them, and re-layouts: 29.7 us -> none  [the longest x12 27.4 us: record_spectra(): jnp.concatenate([jnp.zeros((row_total, half_lag), jnp.bfloat16), records,...]
  transfers between devices with their start and end apart: 8 -> 0, of which waited for: 2 -> 0; matrix products, arithmetic and copies ran while one was open for 6% -> 0% of each run, Pallas kernels for 0% -> 0%
where the time goes in v1:
time: 175 us
  blocking collectives  84.7 us (48%)
  Pallas kernels  81 us (46%)
  local copies, waits for them, and re-layouts  7.02 us (4%)
    psum x1, blocking collectives, local(): stack = lax.psum(part, ('grp', 'dev')) / math.sqrt(CH * shape[0] * shape[1])  84.7 us
    pallas_call x1, Pallas kernels, local(): pl.pallas_call(functools.partial(kernel, shape), out_shape=(jax.ShapeDtyp...  81 us
    unnamed x17, local copies, waits for them, and re-layouts  6.83 us

profile of v1, /device:TPU:1, one launch (start us, length us, event | category | flops | bytes accessed | tf_op | source)
XLA Modules:
  0.0 174.7 jit_solution(9529332009429051908)
XLA Ops:
  0.6 0.0 copy-start.6
  0.6 0.7 convert_element_type.8
  1.3 0.0 copy-done.6
  1.3 0.1 broadcast_in_dim.2.offv
  1.4 0.1 copy.11
  1.5 0.0 copy-start.7
  1.5 0.7 copy-done.7
  2.2 0.0 copy-start.5
  2.3 0.7 copy-done.5
  2.9 0.0 copy-start
  2.9 1.1 copy-done
  4.1 0.0 copy-start.1
  4.1 0.9 copy-done.1
  5.0 0.0 copy-start.2
  5.0 0.9 copy-done.2
  5.9 0.0 copy-start.3
  5.9 0.9 copy-done.3
  6.8 0.0 copy-start.4
  6.8 0.9 copy-done.4
  7.7 81.0 %whiten_correlate.1 = (f32[64,8,128]{2,1,0:T(8,128)S(1)}, f32[8,128]{1,0:T(8,128)S(1)}) custom-call(bf16[6,64,1024]{2,1,0:T(8,128)(2,1)S(1)} %bitcast.2, f32[64,128]{1,0:T(8,128)S(1)} %pad_convert_fusion.taps, bf16[64,128]{1,0:T(8,128)(2,1)S(1)} %pad.12.keepv, s32[6,64]{1,0:T(8,128)S(1)} %bitcast.3, s32[8]{0:T(128)S(1)} %copy-done.6, ...), custom_call_target="tpu_custom_call" | custom-call | tf_op jit(solution)/shard_map/whiten_correlate/pallas_call | solution.py:311
  88.7 84.7 %psum.7 = f32[8,128]{1,0:T(8,128)S(1)} all-reduce(f32[8,128]{1,0:T(8,128)S(1)} %get-tuple-element.5), channel_id=1, replica_groups=mesh['grp'=16,'dev'=16] {'grp','dev'}, use_global_device_ids=true, to_apply=%region_0.1 | all-reduce | flops 1024 | bytes 8192 | tf_op jit(solution)/shard_map/psum | solution.py:346
  173.4 0.6 broadcast_multiply_fusion
  174.0 0.7 copy.13
  (2 shorter events, 0.0 us)
Async XLA Ops:
  0.6 0.7 copy-start.6
  1.5 0.7 copy-start.7
  2.2 0.7 copy-start.5
  2.9 1.1 copy-start
  4.1 0.9 copy-start.1
  5.0 0.9 copy-start.2
  5.9 0.9 copy-start.3
  6.8 0.9 copy-start.4

commit v2 on v1

v2 whole, which is shorter than its diff:
```python
import functools
import math

import jax
import jax.numpy as jnp
import numpy as np
from jax import lax
from jax.experimental import pallas as pl
from jax.experimental.pallas import tpu as pltpu
from jax.sharding import PartitionSpec as P

SEG = 6
SAMP = 1024
BLK = 128
TAPS = 64
NLAG = 128
NOFF = 8
CH = 64
NB = SAMP // BLK
NEAR = 3 * CH
EXT = 5 * CH
GRP_CH = 16
ROWS = NB * CH
PAD_ROWS = ROWS + 2 * CH
QUART = 4
MESH = pl.DeviceIdType.MESH


def dft_tables():
    n = np.arange(2 * BLK, dtype=np.float64)[:, None]
    f = np.arange(BLK, dtype=np.float64)[None, :] + 0.5
    ang = 2.0 * np.pi * f * n / (2 * BLK)
    full = np.concatenate([np.cos(ang), -np.sin(ang)], axis=1)
    half = BLK // 2
    own = full[:BLK]
    win = np.concatenate([full[half : half + BLK], full[half + BLK :], full[:half]], axis=0)

    def split(t):
        t32 = t.astype(np.float32)
        hi = t32.astype(jnp.bfloat16)
        lo = (t32 - hi.astype(np.float32)).astype(jnp.bfloat16)
        return hi, lo

    own_hi, own_lo = split(own)
    win_hi, win_lo = split(win)
    m = np.arange(NLAG, dtype=np.float64)[None, :]
    ang_inv = 2.0 * np.pi * f.T * m / (2 * BLK)
    inv = np.concatenate([np.cos(ang_inv), -np.sin(ang_inv)], axis=0) / BLK
    return (
        np.concatenate([own_hi, own_lo], axis=0),
        np.concatenate([win_hi, win_lo], axis=0),
        inv.astype(np.float32),
    )


def kernel(
    shape,
    ser_hbm,
    tk,
    offs,
    own_hbm,
    win_hbm,
    inv_hbm,
    out,
    stack,
    ser,
    t_own,
    t_win,
    t_inv,
    white,
    p1,
    p2,
    m2,
    kv,
    k1,
    k2,
    km2,
    scr,
    keep_near,
    keep_left,
    xr,
    xi,
    yr,
    yi,
    accr,
    acci,
    cnt,
    res,
    res_send,
    res_recv,
    part,
    got_a,
    got_b,
    ssem,
    rsem,
    asem,
    bsem,
    lsem,
):
    ng, nd = shape
    f32, b16 = jnp.float32, jnp.bfloat16
    me_g, me_d = lax.axis_index("grp"), lax.axis_index("dev")

    def dev(k):
        t = lax.rem(me_g * nd + me_d + (k + ng * nd), ng * nd)
        return (t // nd, lax.rem(t, nd))

    def along_dev(k):
        return (me_g, lax.rem(me_d + k, nd))

    def along_grp(k):
        return (lax.rem(me_g + k, ng), me_d)

    loads = [
        pltpu.make_async_copy(
            ser_hbm.at[:, pl.ds(g * GRP_CH, GRP_CH), :],
            ser.at[:, pl.ds(g * GRP_CH, GRP_CH), :],
            lsem.at[g],
        )
        for g in range(CH // GRP_CH)
    ]
    loads += [
        pltpu.make_async_copy(own_hbm, t_own, lsem.at[4]),
        pltpu.make_async_copy(win_hbm, t_win, lsem.at[5]),
        pltpu.make_async_copy(inv_hbm, t_inv, lsem.at[6]),
    ]
    for copy in loads:
        copy.start()

    bar = pltpu.get_barrier_semaphore()
    for k in (-2, -1, 1, 2):
        pl.semaphore_signal(bar, inc=1, device_id=dev(k), device_id_type=MESH)
    for k in range(1, nd):
        pl.semaphore_signal(bar, inc=1, device_id=along_dev(k), device_id_type=MESH)
    for k in range(1, ng):
        pl.semaphore_signal(bar, inc=1, device_id=along_grp(k), device_id_type=MESH)

    for s in range(SEG):
        scr[pl.ds(s * 9 * GRP_CH, GRP_CH), :] = jnp.zeros((GRP_CH, BLK), f32)
        for ref in (white, p1, p2):
            ref[s, pl.ds(0, CH), :] = jnp.zeros((CH, BLK), b16)
            ref[s, pl.ds(ROWS + CH, CH), :] = jnp.zeros((CH, BLK), b16)
    accr[...] = jnp.zeros_like(accr)
    acci[...] = jnp.zeros_like(acci)

    lane = lax.broadcasted_iota(jnp.int32, (CH, BLK), 1)
    kv[...] = jnp.where(lane < TAPS, 0.0, tk[...]).astype(b16)

    row_i = lax.broadcasted_iota(jnp.int32, (BLK, BLK), 0)
    col_i = lax.broadcasted_iota(jnp.int32, (BLK, BLK), 1)
    causal = col_i >= row_i
    row_lane = lax.broadcasted_iota(jnp.int32, (1, BLK), 1)

    for g in range(CH // GRP_CH):
        loads[g].wait()
        for s in range(SEG):
            for b in range(NB):
                x = ser[s, pl.ds(g * GRP_CH, GRP_CH), pl.ds(b * BLK, BLK)]
                scr[pl.ds((s * 9 + b + 1) * GRP_CH, GRP_CH), :] = x.astype(f32)

        @pl.loop(0, GRP_CH, unroll=2)
        def _(c):
            cur = [scr[pl.ds((s * 9 + 1) * GRP_CH + c, NB, stride=GRP_CH), :] for s in range(SEG)]
            prv = [scr[pl.ds(s * 9 * GRP_CH + c, NB, stride=GRP_CH), :] for s in range(SEG)]
            x = jnp.concatenate(
                [jnp.concatenate(prv, axis=0), jnp.concatenate(cur, axis=0)], axis=1
            ).astype(b16)
            row = jnp.where(row_lane < TAPS, tk[pl.ds(g * GRP_CH + c, 1), :], 0.0)
            circ = pltpu.roll(jnp.broadcast_to(row, (BLK, BLK)), 0, 1, stride=1, stride_axis=0)
            toep = jnp.concatenate(
                [jnp.where(causal, 0.0, circ), jnp.where(causal, circ, 0.0)], axis=0
            ).astype(b16)
            y = jnp.dot(x, toep, preferred_element_type=f32)
            for s in range(SEG):
                scr[pl.ds((s * 9 + 1) * GRP_CH + c, NB, stride=GRP_CH), :] = y[s * NB : (s + 1) * NB]

        flags = tk[pl.ds(g * GRP_CH, GRP_CH), :]
        for s in range(SEG):
            flag = jnp.broadcast_to(flags[:, TAPS + s : TAPS + s + 1], (GRP_CH, BLK))
            for b in range(NB):
                y = scr[pl.ds((s * 9 + b + 1) * GRP_CH, GRP_CH), :] * flag
                white[s, pl.ds((b + 1) * CH + g * GRP_CH, GRP_CH), :] = y.astype(b16)

    def remote(src, dst, line, at, to):
        return pltpu.make_async_remote_copy(
            src_ref=src,
            dst_ref=dst,
            send_sem=ssem.at[line, at],
            recv_sem=rsem.at[line, at],
            device_id=dev(to),
            device_id_type=MESH,
        )

    def keep_copy(line):
        if line == 0:
            return remote(kv, k1, 0, SEG, -1)
        if line == 1:
            return remote(k1, k2, 1, SEG, -1)
        return remote(kv, km2, 2, SEG, 2)

    def seg_copy(line, s):
        body = pl.ds(CH, ROWS)
        if line == 0:
            return remote(white.at[s, body], p1.at[s, body], 0, s, -1)
        if line == 1:
            return remote(p1.at[s, body], p2.at[s, body], 1, s, -1)
        return remote(white.at[s, body], m2.at[s], 2, s, 2)

    def window_dft(src, s, bases):
        nxt = jnp.where(row_lane < BLK // 2, 1.0, 0.0).astype(b16)
        prv = jnp.where(row_lane < BLK // 2, 0.0, 1.0).astype(b16)
        cur = src[s, pl.ds(CH, ROWS), :]
        mix = src[s, pl.ds(2 * CH, ROWS), :] * nxt + src[s, pl.ds(0, ROWS), :] * prv
        x = jnp.concatenate([cur, mix, cur, mix], axis=1)
        y = jnp.dot(x, t_win[...], preferred_element_type=f32)
        for b in range(NB):
            for base in bases:
                yr[pl.ds(b * EXT + base, CH), :] = y[b * CH : (b + 1) * CH, :BLK]
                yi[pl.ds(b * EXT + base, CH), :] = y[b * CH : (b + 1) * CH, BLK:]

    def own_dft(src, s, start, base):
        w = src[s, pl.ds(start, ROWS), :]
        y = jnp.dot(jnp.concatenate([w, w], axis=1), t_own[...], preferred_element_type=f32)
        for b in range(NB):
            xr[pl.ds(b * 2 * CH + base, CH), :] = y[b * CH : (b + 1) * CH, :BLK]
            xi[pl.ds(b * 2 * CH + base, CH), :] = y[b * CH : (b + 1) * CH, BLK:]

    eight = lax.broadcasted_iota(jnp.int32, (8, BLK), 0)

    def away(j, r0):
        return eight + (r0 + offs[j]) >= NEAR

    def pairs(g):
        r0 = pl.multiple_of(g * 8, 8)
        far = [away(j, r0) for j in range(NOFF)]
        tr = [accr[pl.ds(j * CH + r0, 8), :] for j in range(NOFF)]
        ti = [acci[pl.ds(j * CH + r0, 8), :] for j in range(NOFF)]
        for b in range(NB):
            ar = xr[pl.ds(b * 2 * CH + r0, 8), :]
            ai = xi[pl.ds(b * 2 * CH + r0, 8), :]
            cr = xr[pl.ds(b * 2 * CH + CH + r0, 8), :]
            ci = xi[pl.ds(b * 2 * CH + CH + r0, 8), :]
            for j in range(NOFF):
                near = pl.ds(b * EXT + r0 + offs[j], 8)
                br = yr[near, :]
                bi = yi[near, :]
                lr = jnp.where(far[j], cr, ar)
                li = jnp.where(far[j], ci, ai)
                tr[j] = tr[j] + (lr * br + li * bi)
                ti[j] = ti[j] + (lr * bi - li * br)
        for j in range(NOFF):
            accr[pl.ds(j * CH + r0, 8), :] = tr[j]
            acci[pl.ds(j * CH + r0, 8), :] = ti[j]

    def first_dfts(s):
        own_dft(white, s, CH, 0)
        window_dft(white, s, (0,))
        window_dft(p1, s, (CH, 3 * CH))

    def last_dfts(s):
        own_dft(m2, s, 0, CH)
        window_dft(p2, s, (2 * CH, 4 * CH))

    pl.semaphore_wait(bar, 4 + (nd - 1) + (ng - 1))
    keep_copy(0).start()
    keep_copy(2).start()
    seg_copy(0, 0).start()
    seg_copy(0, 1).start()
    for s in range(SEG):
        seg_copy(2, s).start()
    keep_copy(0).wait_recv()
    keep_copy(1).start()
    for copy in loads[4:]:
        copy.wait()

    @pl.loop(0, SEG)
    def _(s):
        seg_copy(0, s).wait_recv()
        seg_copy(1, s).start()

        @pl.when(s < SEG - 2)
        def _():
            seg_copy(0, s + 2).start()

        @pl.when(s > 0)
        def _():
            seg_copy(1, s - 1).wait_recv()
            seg_copy(2, s - 1).wait_recv()
            last_dfts(s - 1)

            @pl.loop(0, CH // 8)
            def _(g):
                pairs(g)

        first_dfts(s)

    keep_copy(1).wait_recv()
    keep_copy(2).wait_recv()
    keep_left[pl.ds(0, CH), :] = kv[...].astype(f32)
    keep_left[pl.ds(CH, CH), :] = km2[...].astype(f32)
    keep_near[pl.ds(0, CH), :] = kv[...].astype(f32)
    for base in (CH, 3 * CH):
        keep_near[pl.ds(base, CH), :] = k1[...].astype(f32)
    for base in (2 * CH, 4 * CH):
        keep_near[pl.ds(base, CH), :] = k2[...].astype(f32)

    @pl.loop(0, CH // 8)
    def _(g):
        r0 = pl.multiple_of(g * 8, 8)
        a = keep_left[pl.ds(r0, 8), :]
        c = keep_left[pl.ds(CH + r0, 8), :]
        for j in range(NOFF):
            near = keep_near[pl.ds(r0 + offs[j], 8), :]
            cnt[pl.ds(j * CH + r0, 8), :] = jnp.where(away(j, r0), c, a) * near

    ones = jnp.ones((BLK, BLK), b16)
    per = CH // QUART

    def back_copy(q):
        rows = pl.ds(q * per * NOFF, per * NOFF)
        return remote(res_send.at[rows], res_recv.at[rows], 3, q, -2)

    seg_copy(1, SEG - 1).wait_recv()
    seg_copy(2, SEG - 1).wait_recv()
    last_dfts(SEG - 1)

    part[...] = jnp.zeros((NOFF, NLAG), f32)
    for q in range(QUART):

        @pl.loop(q * per // 8, (q + 1) * per // 8)
        def _(g):
            pairs(g)

        rows = [pl.ds(j * CH + q * per, per) for j in range(NOFF)]
        spec = jnp.concatenate(
            [
                jnp.concatenate([accr[r, :] for r in rows], axis=0),
                jnp.concatenate([acci[r, :] for r in rows], axis=0),
            ],
            axis=1,
        )
        lag = jnp.dot(spec, t_inv[...], precision=lax.Precision.HIGHEST, preferred_element_type=f32)
        both = jnp.concatenate([cnt[r, :] for r in rows], axis=0).astype(b16)
        number = jnp.dot(both, ones, preferred_element_type=f32)
        corr = lag / (jnp.maximum(number, 1.0) * math.sqrt(SAMP))
        at = pl.ds(q * per * NOFF, per * NOFF)
        res[at, :] = corr
        res_send[at, :] = corr.astype(b16)
        back_copy(q).start()
        part[...] += jnp.concatenate(
            [jnp.sum(corr[j * per : (j + 1) * per], axis=0, keepdims=True) for j in range(NOFF)],
            axis=0,
        )

    def sum_copy(src, got, sem, k, to):
        return pltpu.make_async_remote_copy(
            src_ref=src,
            dst_ref=got.at[k],
            send_sem=sem.at[0, k],
            recv_sem=sem.at[1, k],
            device_id=to,
            device_id_type=MESH,
        )

    for k in range(1, nd):
        sum_copy(part, got_a, asem, k, along_dev(k)).start()
    got_a[0] = part[...]
    for k in range(1, nd):
        sum_copy(part, got_a, asem, k, along_dev(k)).wait_recv()
    got_b[0] = jnp.sum(got_a[...], axis=0)
    for k in range(1, ng):
        sum_copy(got_b.at[0], got_b, bsem, k, along_grp(k)).start()

    for q in range(QUART):
        back_copy(q).wait_recv()
        for j in range(NOFF):
            at = pl.ds((q * NOFF + j) * per, per)
            mine = res[at, :]
            theirs = res_recv[at, :].astype(f32)
            for h in range(per // 8):
                r0 = q * per + h * 8
                val = jnp.where(away(j, r0), theirs[h * 8 : h * 8 + 8], mine[h * 8 : h * 8 + 8])
                out[pl.ds(r0 * NOFF + j, 8, stride=NOFF), :] = val

    for k in range(1, ng):
        sum_copy(got_b.at[0], got_b, bsem, k, along_grp(k)).wait_recv()
    stack[...] = jnp.sum(got_b[...], axis=0) * (1.0 / math.sqrt(CH * nd * ng))

    for k in range(1, nd):
        sum_copy(part, got_a, asem, k, along_dev(k)).wait_send()
    for k in range(1, ng):
        sum_copy(got_b.at[0], got_b, bsem, k, along_grp(k)).wait_send()
    for q in range(QUART):
        back_copy(q).wait_send()

    @pl.loop(0, SEG)
    def _(s):
        for line in range(3):
            seg_copy(line, s).wait_send()

    for line in range(3):
        keep_copy(line).wait_send()


def local(shape, series, taps, keep, offsets):
    ng, nd = shape
    f32, b16 = jnp.float32, jnp.bfloat16
    ser = jnp.transpose(series, (1, 0, 2))
    tk = jnp.concatenate(
        [taps.astype(f32), keep.astype(f32), jnp.zeros((CH, BLK - TAPS - SEG), f32)], axis=1
    )
    vmem = pl.BlockSpec(memory_space=pltpu.VMEM)
    smem = pl.BlockSpec(memory_space=pltpu.SMEM)
    hbm = pl.BlockSpec(memory_space=pltpu.HBM)
    pairs = CH * NOFF
    vm = pltpu.VMEM
    corr, stack = pl.pallas_call(
        functools.partial(kernel, shape),
        out_shape=(
            jax.ShapeDtypeStruct((pairs, NLAG), f32),
            jax.ShapeDtypeStruct((NOFF, NLAG), f32),
        ),
        in_specs=[hbm, vmem, smem, hbm, hbm, hbm],
        out_specs=(vmem, vmem),
        scratch_shapes=[
            vm((SEG, CH, SAMP), b16),
            vm((2 * BLK, 2 * BLK), b16),
            vm((4 * BLK, 2 * BLK), b16),
            vm((2 * BLK, NLAG), f32),
            vm((SEG, PAD_ROWS, BLK), b16),
            vm((SEG, PAD_ROWS, BLK), b16),
            vm((SEG, PAD_ROWS, BLK), b16),
            vm((SEG, ROWS, BLK), b16),
            vm((CH, BLK), b16),
            vm((CH, BLK), b16),
            vm((CH, BLK), b16),
            vm((CH, BLK), b16),
            vm((SEG * 9 * GRP_CH, BLK), f32),
            vm((EXT, BLK), f32),
            vm((2 * CH, BLK), f32),
            vm((NB * 2 * CH, BLK), f32),
            vm((NB * 2 * CH, BLK), f32),
            vm((NB * EXT, BLK), f32),
            vm((NB * EXT, BLK), f32),
            vm((pairs, BLK), f32),
            vm((pairs, BLK), f32),
            vm((pairs, BLK), f32),
            vm((pairs, NLAG), f32),
            vm((pairs, NLAG), b16),
            vm((pairs, NLAG), b16),
            vm((NOFF, NLAG), f32),
            vm((nd, NOFF, NLAG), f32),
            vm((ng, NOFF, NLAG), f32),
            pltpu.SemaphoreType.DMA((4, SEG + 1)),
            pltpu.SemaphoreType.DMA((4, SEG + 1)),
            pltpu.SemaphoreType.DMA((2, nd)),
            pltpu.SemaphoreType.DMA((2, ng)),
            pltpu.SemaphoreType.DMA((7,)),
        ],
        compiler_params=pltpu.CompilerParams(
            collective_id=0, has_side_effects=True, vmem_limit_bytes=48 << 20
        ),
        name="whiten_correlate",
    )(ser, tk, offsets, *dft_tables())
    return corr.reshape(CH, NOFF, NLAG), stack


def solution(mesh):
    spec3 = P(("grp", "dev"), None, None)
    spec2 = P(("grp", "dev"), None)
    shape = (mesh.shape["grp"], mesh.shape["dev"])
    return jax.shard_map(
        functools.partial(local, shape),
        mesh=mesh,
        in_specs=(spec3, spec2, spec2, P()),
        out_specs=(spec3, P()),
        check_vma=False,
    )
```

time: 175 us -> 81.1 us (0.46)
  blocking collectives: 84.7 us -> 0 us
  Pallas kernels: 81 us -> 73.7 us
  local copies, waits for them, and re-layouts: 7.02 us -> 5.04 us
    psum x1 -> x0, blocking collectives: 84.7 us -> none  [local(): stack = lax.psum(part, ('grp', 'dev')) / math.sqrt(CH * shape[0] * shape[1])]
    pallas_call x1, Pallas kernels: 81 us -> 73.7 us  [local(): pl.pallas_call(functools.partial(kernel, shape), out_shape=(jax.ShapeDtyp...]
    unnamed x17 -> x12, local copies, waits for them, and re-layouts: 6.83 us -> 4.86 us
where the time goes in v2:
time: 81.1 us; the launch traced here: 80.8 us
  Pallas kernels  73.7 us (91%)
  local copies, waits for them, and re-layouts  5.04 us (6%)
  other arithmetic  1.49 us (2%)
    pallas_call x1, Pallas kernels, local(): pl.pallas_call(functools.partial(kernel, shape), out_shape=(jax.ShapeDtyp...  73.7 us
    unnamed x12, local copies, waits for them, and re-layouts  4.86 us

profile of v2, /device:TPU:1, one launch (start us, length us, event | category | flops | bytes accessed | tf_op | source)
XLA Modules:
  0.0 80.8 jit_solution(9572983136925483568)
XLA Ops:
  0.6 0.0 copy-start.2
  0.7 0.1 pad.2.clone
  0.7 0.7 convert_element_type.7
  1.4 0.1 copy.9
  1.5 0.7 convert_element_type.6
  2.2 0.0 copy-start.4
  2.2 0.1 maximum_maximum_fusion.tk
  2.3 0.0 copy-done.2
  2.3 0.6 copy-done.4
  2.9 0.0 copy-start
  2.9 1.1 %copy-done = bf16[64,6,1024]{2,0,1:T(8,128)(2,1)S(1)} copy-done((bf16[64,6,1024]{2,0,1:T(8,128)(2,1)S(1)}, bf16[64,6,1024]{2,0,1:T(8,128)(2,1)}, u32[]{:S(2)}) %copy-start) | copy-done | bytes 786456
  4.0 0.0 copy-start.1
  4.0 0.9 %copy-done.1 = bf16[512,256]{1,0:T(8,128)(2,1)S(1)} copy-done((bf16[512,256]{1,0:T(8,128)(2,1)S(1)}, bf16[512,256]{1,0:T(8,128)(2,1)}, u32[]{:S(2)}) %copy-start.1) | copy-done | bytes 262168
  5.0 0.0 copy-start.3
  5.0 0.9 %copy-done.3 = bf16[256,256]{1,0:T(8,128)(2,1)S(1)} copy-done((bf16[256,256]{1,0:T(8,128)(2,1)S(1)}, bf16[256,256]{1,0:T(8,128)(2,1)}, u32[]{:S(2)}) %copy-start.3) | copy-done | bytes 131096
  5.9 73.7 %whiten_correlate.1 = (f32[512,128]{1,0:T(8,128)S(1)}, f32[8,128]{1,0:T(8,128)S(1)}) custom-call(bf16[6,64,1024]{2,1,0:T(8,128)(2,1)S(1)} %bitcast.2, f32[64,128]{1,0:T(8,128)S(1)} %maximum_maximum_fusion.tk, s32[8]{0:T(128)S(1)} %copy-done.4, bf16[256,256]{1,0:T(8,128)(2,1)S(1)} %copy-done.3, bf16[512,256]{1,0:T(8,128)(2,1)S(1)} %copy-done.1, ...), custom_call_target="tpu_custom_call" | custom-call | tf_op jit(solution)/shard_map/whiten_correlate/pallas_call | solution.py:417
  79.6 0.7 copy.12
  80.3 0.6 copy.13
  (1 shorter events, 0.0 us)
Async XLA Ops:
  0.6 1.7 %copy-start.2 = (f32[256,128]{1,0:T(8,128)S(1)}, f32[256,128]{1,0:T(8,128)}, u32[]{:S(2)}) copy-start(f32[256,128]{1,0:T(8,128)} %constant.10.clone.inv_hbm) | copy-start | bytes 393220
  2.2 0.7 copy-start.4
  2.9 1.1 %copy-start = (bf16[64,6,1024]{2,0,1:T(8,128)(2,1)S(1)}, bf16[64,6,1024]{2,0,1:T(8,128)(2,1)}, u32[]{:S(2)}) copy-start(bf16[64,6,1024]{2,0,1:T(8,128)(2,1)} %param.7) | copy-start | bytes 2359300
  4.0 0.9 %copy-start.1 = (bf16[512,256]{1,0:T(8,128)(2,1)S(1)}, bf16[512,256]{1,0:T(8,128)(2,1)}, u32[]{:S(2)}) copy-start(bf16[512,256]{1,0:T(8,128)(2,1)} %constant.9.clone.win_hbm) | copy-start | bytes 786436
  5.0 0.9 %copy-start.3 = (bf16[256,256]{1,0:T(8,128)(2,1)S(1)}, bf16[256,256]{1,0:T(8,128)(2,1)}, u32[]{:S(2)}) copy-start(bf16[256,256]{1,0:T(8,128)(2,1)} %constant.8.clone.own_hbm) | copy-start | bytes 393220

commit v3 on v2

v3 whole, which is shorter than its diff:
```python
import functools
import math

import jax
import jax.numpy as jnp
import numpy as np
from jax import lax
from jax.experimental import pallas as pl
from jax.experimental.pallas import tpu as pltpu
from jax.sharding import PartitionSpec as P

SEG = 6
SAMP = 1024
BLK = 128
TAPS = 64
NLAG = 128
NOFF = 8
CH = 64
NB = SAMP // BLK
NEAR = 3 * CH
EXT = 5 * CH
GRP_CH = 16
ROWS = NB * CH
EARLY = 3
QUART = 4
MESH = pl.DeviceIdType.MESH


def split(t):
    t32 = t.astype(np.float32)
    hi = t32.astype(jnp.bfloat16)
    lo = (t32 - hi.astype(np.float32)).astype(jnp.bfloat16)
    return hi, lo


def dft_tables():
    n = np.arange(2 * BLK, dtype=np.float64)[:, None]
    f = np.arange(BLK, dtype=np.float64)[None, :] + 0.5
    ang = 2.0 * np.pi * f * n / (2 * BLK)
    full = np.concatenate([np.cos(ang), -np.sin(ang)], axis=1)
    half = BLK // 2
    own = full[:BLK]
    win = np.concatenate([full[half : half + BLK], full[half + BLK :], full[:half]], axis=0)
    m = np.arange(NLAG, dtype=np.float64)[None, :]
    ang_inv = 2.0 * np.pi * f.T * m / (2 * BLK)
    inv_hi, inv_lo = split(np.concatenate([np.cos(ang_inv), -np.sin(ang_inv)], axis=0) / BLK)
    inv = np.concatenate(
        [
            np.concatenate([inv_hi, inv_lo], axis=1),
            np.concatenate([inv_hi, np.zeros_like(inv_lo)], axis=1),
        ],
        axis=0,
    )
    return np.concatenate(split(own), axis=0), np.concatenate(split(win), axis=0), inv


def kernel(
    shape,
    ser_hbm,
    taps_hbm,
    keep_hbm,
    offs,
    own_hbm,
    win_hbm,
    inv_hbm,
    out,
    stack,
    ser,
    taps_in,
    keep_in,
    t_own,
    t_win,
    t_inv,
    white,
    p1,
    p2,
    m2,
    kv,
    k1,
    k2,
    km2,
    kt,
    tk,
    scr,
    keep_near,
    keep_left,
    xr,
    xi,
    yr,
    yi,
    accr,
    acci,
    scale,
    res,
    res_send,
    res_recv,
    part,
    got_a,
    got_b,
    ssem,
    rsem,
    asem,
    bsem,
    lsem,
):
    ng, nd = shape
    f32, b16 = jnp.float32, jnp.bfloat16
    me_g, me_d = lax.axis_index("grp"), lax.axis_index("dev")

    def dev(k):
        t = lax.rem(me_g * nd + me_d + (k + ng * nd), ng * nd)
        return (t // nd, lax.rem(t, nd))

    def along_dev(k):
        return (me_g, lax.rem(me_d + k, nd))

    def along_grp(k):
        return (lax.rem(me_g + k, ng), me_d)

    bar = pltpu.get_barrier_semaphore()
    for k in (-2, -1, 1, 2):
        pl.semaphore_signal(bar, inc=1, device_id=dev(k), device_id_type=MESH)

    groups = CH // GRP_CH
    small = [
        pltpu.make_async_copy(taps_hbm, taps_in, lsem.at[groups]),
        pltpu.make_async_copy(keep_hbm, keep_in, lsem.at[groups + 1]),
    ]
    loads = [
        pltpu.make_async_copy(
            ser_hbm.at[:, pl.ds(g * GRP_CH, GRP_CH), :],
            ser.at[:, pl.ds(g * GRP_CH, GRP_CH), :],
            lsem.at[g],
        )
        for g in range(groups)
    ]
    tables = [
        pltpu.make_async_copy(src, dst, lsem.at[groups + 2 + i])
        for i, (src, dst) in enumerate(((own_hbm, t_own), (win_hbm, t_win), (inv_hbm, t_inv)))
    ]
    for copy in small + loads + tables:
        copy.start()

    for k in range(1, nd):
        pl.semaphore_signal(bar, inc=1, device_id=along_dev(k), device_id_type=MESH)
    for k in range(1, ng):
        pl.semaphore_signal(bar, inc=1, device_id=along_grp(k), device_id_type=MESH)

    kt[...] = jnp.zeros_like(kt)
    tk[...] = jnp.zeros_like(tk)
    for s in range(SEG):
        scr[pl.ds(s * 9 * GRP_CH, GRP_CH), :] = jnp.zeros((GRP_CH, BLK), f32)
    for copy in small:
        copy.wait()
    tk[:, pl.ds(0, TAPS)] = taps_in[...].astype(f32)
    kt[pl.ds(0, SEG), pl.ds(0, CH)] = keep_in[...].astype(f32)
    flags = jnp.transpose(kt[...])[:CH]
    keep_left[pl.ds(0, CH), :] = flags
    kv[...] = flags.astype(b16)

    def remote(src, dst, line, at, to):
        return pltpu.make_async_remote_copy(
            src_ref=src,
            dst_ref=dst,
            send_sem=ssem.at[line, at],
            recv_sem=rsem.at[line, at],
            device_id=dev(to),
            device_id_type=MESH,
        )

    def keep_copy(line):
        if line == 0:
            return remote(kv, k1, 0, SEG, -1)
        if line == 1:
            return remote(k1, k2, 1, SEG, -1)
        return remote(kv, km2, 2, SEG, 2)

    def seg_copy(line, s, first=0, count=CH):
        blocks, rows = pl.ds(1, NB), pl.ds(first, count)
        if line == 0:
            return remote(white.at[s, blocks, rows], p1.at[s, blocks, rows], 0, s, -1)
        if line == 1:
            return remote(p1.at[s, blocks, rows], p2.at[s, blocks, rows], 1, s, -1)
        return remote(white.at[s, blocks, rows], m2.at[s, :, rows], 2, s, 2)

    row_i = lax.broadcasted_iota(jnp.int32, (BLK, BLK), 0)
    col_i = lax.broadcasted_iota(jnp.int32, (BLK, BLK), 1)
    causal = col_i >= row_i
    row_lane = lax.broadcasted_iota(jnp.int32, (1, BLK), 1)

    for g in range(groups):
        loads[g].wait()
        for s in range(SEG):
            for b in range(NB):
                x = ser[s, pl.ds(g * GRP_CH, GRP_CH), pl.ds(b * BLK, BLK)]
                scr[pl.ds((s * 9 + b + 1) * GRP_CH, GRP_CH), :] = x.astype(f32)

        @pl.loop(0, GRP_CH, unroll=2)
        def _(c):
            cur = [scr[pl.ds((s * 9 + 1) * GRP_CH + c, NB, stride=GRP_CH), :] for s in range(SEG)]
            prv = [scr[pl.ds(s * 9 * GRP_CH + c, NB, stride=GRP_CH), :] for s in range(SEG)]
            x = jnp.concatenate(
                [jnp.concatenate(prv, axis=0), jnp.concatenate(cur, axis=0)], axis=1
            ).astype(b16)
            row = tk[pl.ds(g * GRP_CH + c, 1), :]
            circ = pltpu.roll(jnp.broadcast_to(row, (BLK, BLK)), 0, 1, stride=1, stride_axis=0)
            toep = jnp.concatenate(
                [jnp.where(causal, 0.0, circ), jnp.where(causal, circ, 0.0)], axis=0
            ).astype(b16)
            y = jnp.dot(x, toep, preferred_element_type=f32)
            for s in range(SEG):
                scr[pl.ds((s * 9 + 1) * GRP_CH + c, NB, stride=GRP_CH), :] = y[s * NB : (s + 1) * NB]

        mine = keep_left[pl.ds(g * GRP_CH, GRP_CH), :]
        for s in range(SEG):
            flag = jnp.broadcast_to(mine[:, s : s + 1], (GRP_CH, BLK))
            for b in range(NB):
                y = scr[pl.ds((s * 9 + b + 1) * GRP_CH, GRP_CH), :] * flag
                white[s, b + 1, pl.ds(g * GRP_CH, GRP_CH), :] = y.astype(b16)
        if g == 0:
            pl.semaphore_wait(bar, 4 + (nd - 1) + (ng - 1))
            keep_copy(0).start()
            keep_copy(2).start()
        for s in range(EARLY):
            seg_copy(0, s, g * GRP_CH, GRP_CH).start()
            seg_copy(2, s, g * GRP_CH, GRP_CH).start()

    for s in range(EARLY, SEG):
        seg_copy(2, s).start()
    keep_copy(0).wait_recv()
    keep_copy(1).start()

    for s in range(SEG):
        for ref in (white, p1, p2):
            ref[s, 0] = jnp.zeros((CH, BLK), b16)
            ref[s, NB + 1] = jnp.zeros((CH, BLK), b16)
    accr[...] = jnp.zeros_like(accr)
    acci[...] = jnp.zeros_like(acci)

    def window_dft(src, s, bases):
        nxt = jnp.where(row_lane < BLK // 2, 1.0, 0.0).astype(b16)
        prv = jnp.where(row_lane < BLK // 2, 0.0, 1.0).astype(b16)
        cur = src[s, pl.ds(1, NB)].reshape(ROWS, BLK)
        mix = src[s, pl.ds(2, NB)].reshape(ROWS, BLK) * nxt + src[s, pl.ds(0, NB)].reshape(ROWS, BLK) * prv
        x = jnp.concatenate([cur, mix, cur, mix], axis=1)
        y = jnp.dot(x, t_win[...], preferred_element_type=f32)
        for b in range(NB):
            for base in bases:
                yr[pl.ds(b * EXT + base, CH), :] = y[b * CH : (b + 1) * CH, :BLK]
                yi[pl.ds(b * EXT + base, CH), :] = y[b * CH : (b + 1) * CH, BLK:]

    def own_dft(src, s, start, base):
        w = src[s, pl.ds(start, NB)].reshape(ROWS, BLK)
        y = jnp.dot(jnp.concatenate([w, w], axis=1), t_own[...], preferred_element_type=f32)
        for b in range(NB):
            xr[pl.ds(b * 2 * CH + base, CH), :] = y[b * CH : (b + 1) * CH, :BLK]
            xi[pl.ds(b * 2 * CH + base, CH), :] = y[b * CH : (b + 1) * CH, BLK:]

    eight = lax.broadcasted_iota(jnp.int32, (8, BLK), 0)
    per = CH // QUART

    def away(j, r0):
        return eight + (r0 + offs[j]) >= NEAR

    def slot(g, j):
        first = (g // (per // 8)) * (per * NOFF) + lax.rem(g, per // 8) * 8
        return pl.ds(pl.multiple_of(first + j * per, 8), 8)

    def pair_sums(g):
        r0 = pl.multiple_of(g * 8, 8)
        far = [away(j, r0) for j in range(NOFF)]
        tr = [accr[slot(g, j), :] for j in range(NOFF)]
        ti = [acci[slot(g, j), :] for j in range(NOFF)]
        for b in range(NB):
            ar = xr[pl.ds(b * 2 * CH + r0, 8), :]
            ai = xi[pl.ds(b * 2 * CH + r0, 8), :]
            cr = xr[pl.ds(b * 2 * CH + CH + r0, 8), :]
            ci = xi[pl.ds(b * 2 * CH + CH + r0, 8), :]
            for j in range(NOFF):
                near = pl.ds(b * EXT + r0 + offs[j], 8)
                br = yr[near, :]
                bi = yi[near, :]
                lr = jnp.where(far[j], cr, ar)
                li = jnp.where(far[j], ci, ai)
                tr[j] = tr[j] + (lr * br + li * bi)
                ti[j] = ti[j] + (lr * bi - li * br)
        return tr, ti

    def first_dfts(s):
        own_dft(white, s, 1, 0)
        window_dft(white, s, (0,))
        window_dft(p1, s, (CH, 3 * CH))

    for copy in tables:
        copy.wait()

    @pl.loop(0, SEG)
    def _(s):
        seg_copy(0, s).wait_recv()
        seg_copy(1, s).start()

        @pl.when(s < SEG - EARLY)
        def _():
            seg_copy(0, s + EARLY).start()

        @pl.when(s > 0)
        def _():
            seg_copy(2, s - 1).wait_recv()
            own_dft(m2, s - 1, 0, CH)
            seg_copy(1, s - 1).wait_recv()
            window_dft(p2, s - 1, (2 * CH, 4 * CH))

            @pl.loop(0, CH // 8)
            def _(g):
                tr, ti = pair_sums(g)
                for j in range(NOFF):
                    accr[slot(g, j), :] = tr[j]
                    acci[slot(g, j), :] = ti[j]

        first_dfts(s)

    keep_copy(1).wait_recv()
    keep_copy(2).wait_recv()
    keep_left[pl.ds(CH, CH), :] = km2[...].astype(f32)
    keep_near[pl.ds(0, CH), :] = kv[...].astype(f32)
    for base in (CH, 3 * CH):
        keep_near[pl.ds(base, CH), :] = k1[...].astype(f32)
    for base in (2 * CH, 4 * CH):
        keep_near[pl.ds(base, CH), :] = k2[...].astype(f32)

    @pl.loop(0, CH // 8)
    def _(g):
        r0 = pl.multiple_of(g * 8, 8)
        a = keep_left[pl.ds(r0, 8), :]
        c = keep_left[pl.ds(CH + r0, 8), :]
        for j in range(NOFF):
            near = keep_near[pl.ds(r0 + offs[j], 8), :]
            scale[slot(g, j), :] = jnp.where(away(j, r0), c, a) * near

    ones = jnp.ones((BLK, BLK), b16)
    number = jnp.dot(scale[...].astype(b16), ones, preferred_element_type=f32)
    scale[...] = 1.0 / (jnp.maximum(number, 1.0) * math.sqrt(SAMP))

    def back_copy(q):
        rows = pl.ds(q * per * NOFF, per * NOFF)
        return remote(res_send.at[rows], res_recv.at[rows], 3, q, -2)

    def lags(re, im):
        spec = jnp.concatenate([re, im], axis=1)
        hi = spec.astype(b16)
        lo = (spec - hi.astype(f32)).astype(b16)
        y = jnp.dot(jnp.concatenate([hi, lo], axis=1), t_inv[...], preferred_element_type=f32)
        return y[:, :NLAG] + y[:, NLAG:]

    def sum_copy(src, got, sem, k, to):
        return pltpu.make_async_remote_copy(
            src_ref=src,
            dst_ref=got.at[k],
            send_sem=sem.at[0, k],
            recv_sem=sem.at[1, k],
            device_id=to,
            device_id_type=MESH,
        )

    seg_copy(2, SEG - 1).wait_recv()
    own_dft(m2, SEG - 1, 0, CH)
    seg_copy(1, SEG - 1).wait_recv()
    window_dft(p2, SEG - 1, (2 * CH, 4 * CH))

    def finish(g, sums):
        tr, ti = pair_sums(g)
        new = []
        for j in range(NOFF):
            by = scale[slot(g, j), :]
            tr[j] = tr[j] * by
            ti[j] = ti[j] * by
            accr[slot(g, j), :] = tr[j]
            acci[slot(g, j), :] = ti[j]
        return [t + u for t, u in zip(sums, tr + ti)]

    zero = jnp.zeros((8, BLK), f32)
    sums = lax.fori_loop(0, CH // 8, finish, [zero] * (2 * NOFF))
    sums = [jnp.sum(t, axis=0, keepdims=True) for t in sums]
    part[...] = lags(jnp.concatenate(sums[:NOFF], axis=0), jnp.concatenate(sums[NOFF:], axis=0))
    for k in range(1, ng):
        sum_copy(part, got_a, asem, k, along_grp(k)).start()

    for q in range(QUART):
        at = pl.ds(q * per * NOFF, per * NOFF)
        corr = lags(accr[at, :], acci[at, :])
        res[at, :] = corr
        res_send[at, :] = corr.astype(b16)
        back_copy(q).start()

    got_a[0] = part[...]
    for k in range(1, ng):
        sum_copy(part, got_a, asem, k, along_grp(k)).wait_recv()
    got_b[0] = jnp.sum(got_a[...], axis=0)
    for k in range(1, nd):
        sum_copy(got_b.at[0], got_b, bsem, k, along_dev(k)).start()

    for q in range(QUART):
        back_copy(q).wait_recv()
        for j in range(NOFF):
            at = pl.ds((q * NOFF + j) * per, per)
            mine = res[at, :]
            theirs = res_recv[at, :].astype(f32)
            for h in range(per // 8):
                r0 = q * per + h * 8
                val = jnp.where(away(j, r0), theirs[h * 8 : h * 8 + 8], mine[h * 8 : h * 8 + 8])
                out[pl.ds(r0 * NOFF + j, 8, stride=NOFF), :] = val

    for k in range(1, nd):
        sum_copy(got_b.at[0], got_b, bsem, k, along_dev(k)).wait_recv()
    stack[...] = jnp.sum(got_b[...], axis=0) * (1.0 / math.sqrt(CH * nd * ng))

    for k in range(1, ng):
        sum_copy(part, got_a, asem, k, along_grp(k)).wait_send()
    for k in range(1, nd):
        sum_copy(got_b.at[0], got_b, bsem, k, along_dev(k)).wait_send()
    for q in range(QUART):
        back_copy(q).wait_send()

    @pl.loop(0, SEG)
    def _(s):
        for line in range(3):
            seg_copy(line, s).wait_send()

    for line in range(3):
        keep_copy(line).wait_send()


def local(shape, series, taps, keep, offsets):
    ng, nd = shape
    f32, b16 = jnp.float32, jnp.bfloat16
    ser = jnp.transpose(series, (1, 0, 2))
    keep_rows = jnp.transpose(keep, (1, 0))
    vmem = pl.BlockSpec(memory_space=pltpu.VMEM)
    smem = pl.BlockSpec(memory_space=pltpu.SMEM)
    hbm = pl.BlockSpec(memory_space=pltpu.HBM)
    pairs = CH * NOFF
    vm = pltpu.VMEM
    corr, stack = pl.pallas_call(
        functools.partial(kernel, shape),
        out_shape=(
            jax.ShapeDtypeStruct((pairs, NLAG), f32),
            jax.ShapeDtypeStruct((NOFF, NLAG), f32),
        ),
        in_specs=[hbm, hbm, hbm, smem, hbm, hbm, hbm],
        out_specs=(vmem, vmem),
        scratch_shapes=[
            vm((SEG, CH, SAMP), b16),
            vm((CH, TAPS), b16),
            vm((SEG, CH), jnp.int32),
            vm((2 * BLK, 2 * BLK), b16),
            vm((4 * BLK, 2 * BLK), b16),
            vm((4 * BLK, 2 * NLAG), b16),
            vm((SEG, NB + 2, CH, BLK), b16),
            vm((SEG, NB + 2, CH, BLK), b16),
            vm((SEG, NB + 2, CH, BLK), b16),
            vm((SEG, NB, CH, BLK), b16),
            vm((CH, BLK), b16),
            vm((CH, BLK), b16),
            vm((CH, BLK), b16),
            vm((CH, BLK), b16),
            vm((BLK, BLK), f32),
            vm((CH, BLK), f32),
            vm((SEG * 9 * GRP_CH, BLK), f32),
            vm((EXT, BLK), f32),
            vm((2 * CH, BLK), f32),
            vm((NB * 2 * CH, BLK), f32),
            vm((NB * 2 * CH, BLK), f32),
            vm((NB * EXT, BLK), f32),
            vm((NB * EXT, BLK), f32),
            vm((pairs, BLK), f32),
            vm((pairs, BLK), f32),
            vm((pairs, BLK), f32),
            vm((pairs, NLAG), f32),
            vm((pairs, NLAG), b16),
            vm((pairs, NLAG), b16),
            vm((NOFF, NLAG), f32),
            vm((ng, NOFF, NLAG), f32),
            vm((nd, NOFF, NLAG), f32),
            pltpu.SemaphoreType.DMA((4, SEG + 1)),
            pltpu.SemaphoreType.DMA((4, SEG + 1)),
            pltpu.SemaphoreType.DMA((2, ng)),
            pltpu.SemaphoreType.DMA((2, nd)),
            pltpu.SemaphoreType.DMA((CH // GRP_CH + 5,)),
        ],
        compiler_params=pltpu.CompilerParams(
            collective_id=0, has_side_effects=True, vmem_limit_bytes=60 << 20
        ),
        name="whiten_correlate",
    )(ser, taps, keep_rows, offsets, *dft_tables())
    return corr.reshape(CH, NOFF, NLAG), stack


def solution(mesh):
    spec3 = P(("grp", "dev"), None, None)
    spec2 = P(("grp", "dev"), None)
    shape = (mesh.shape["grp"], mesh.shape["dev"])
    return jax.shard_map(
        functools.partial(local, shape),
        mesh=mesh,
        in_specs=(spec3, spec2, spec2, P()),
        out_specs=(spec3, P()),
        check_vma=False,
    )
```

time: 81.1 us -> 75.1 us (0.926)
  local copies, waits for them, and re-layouts: 5.04 us -> 2.27 us
  Pallas kernels: 73.7 us -> 72 us
  other arithmetic: 1.49 us -> 0 us
    unnamed x12 -> x4, local copies, waits for them, and re-layouts: 4.86 us -> 2.27 us
    pallas_call x1, Pallas kernels: 73.7 us -> 72 us  [local(): pl.pallas_call(functools.partial(kernel, shape), out_shape=(jax.ShapeDtyp...]
    convert_element_type x2 -> x0, other arithmetic: 1.41 us -> none  [the longest x1 0.72 us: local(): taps.astype(f32)]
where the time goes in v3:
time: 75.1 us; the launch traced here: 74.9 us
  Pallas kernels  72 us (96%)
  local copies, waits for them, and re-layouts  2.27 us (3%)
    pallas_call x1, Pallas kernels, local(): pl.pallas_call(functools.partial(kernel, shape), out_shape=(jax.ShapeDtyp...  72 us
    unnamed x4, local copies, waits for them, and re-layouts  2.27 us

profile of v3, /device:TPU:1, one launch (start us, length us, event | category | flops | bytes accessed | tf_op | source)
XLA Modules:
  0.0 74.9 jit_solution(2903449108905962844)
XLA Ops:
  0.6 72.0 %whiten_correlate.1 = (f32[512,128]{1,0:T(8,128)}, f32[8,128]{1,0:T(8,128)}) custom-call(bf16[6,64,1024]{2,1,0:T(8,128)(2,1)} %bitcast.3, bf16[64,64]{1,0:T(8,128)(2,1)} %taps_hbm.1, s32[6,64]{1,0:T(8,128)} %bitcast.5, s32[8]{0:T(128)} %offs.1, bf16[256,256]{1,0:T(8,128)(2,1)} %constant.6.clone.own_hbm, bf16[512,256]{1,0:T(8,128)(2,1)} %constant.7.clone.win_hbm, ...), custom_call_target="tpu_custom_call" | custom-call | tf_op jit(solution)/shard_map/whiten_correlate/pallas_call | solution.py:443
  72.6 0.0 copy-start
  72.6 1.7 %copy.11 = f32[64,8,128]{2,1,0:T(8,128)} copy(f32[64,8,128]{2,1,0:T(8,128)} %bitcast.4) | data formatting | bytes 524288
  74.3 0.0 copy-done
  74.3 0.6 copy.12
Async XLA Ops:
  72.6 1.7 %copy-start = (f32[8,128]{1,0:T(8,128)S(1)}, f32[8,128]{1,0:T(8,128)}, u32[]{:S(2)}) copy-start(f32[8,128]{1,0:T(8,128)} %get-tuple-element.9) | copy-start | bytes 12292

commit v4 on v3

--- a/solution.py
+++ b/solution.py
@@ -21,8 +21,11 @@
 EXT = 5 * CH
 GRP_CH = 16
 ROWS = NB * CH
+QUART = 4
+STAGES = 2
 EARLY = 3
-QUART = 4
+LAG = 2
+PEERS = 16
 MESH = pl.DeviceIdType.MESH
 
 
@@ -94,13 +97,10 @@
     res,
     res_send,
     res_recv,
-    part,
-    got_a,
-    got_b,
+    got,
     ssem,
     rsem,
-    asem,
-    bsem,
+    qsem,
     lsem,
 ):
     ng, nd = shape
@@ -111,11 +111,18 @@
         t = lax.rem(me_g * nd + me_d + (k + ng * nd), ng * nd)
         return (t // nd, lax.rem(t, nd))
 
-    def along_dev(k):
-        return (me_g, lax.rem(me_d + k, nd))
-
-    def along_grp(k):
-        return (lax.rem(me_g + k, ng), me_d)
+    core, my_y = lax.rem(me_g, 2), lax.rem(me_g // 2, 4)
+    x_hi, x_lo = me_g // 8, me_d // 8
+    z = lax.rem(me_d, 8)
+
+    def peer(stage, k):
+        c, yy, xh, xl, zz = core, my_y, x_hi, x_lo, z
+        if stage == 0:
+            yy = lax.rem(my_y + k // 4, 4)
+            xh, xl = lax.rem(x_hi + k // 2 % 2, 2), lax.rem(x_lo + k % 2, 2)
+        else:
+            zz, c = lax.rem(z + k // 2, 8), lax.rem(core + k % 2, 2)
+        return ((xh * 4 + yy) * 2 + c, xl * 8 + zz)
 
     bar = pltpu.get_barrier_semaphore()
     for k in (-2, -1, 1, 2):
@@ -141,10 +148,9 @@
     for copy in small + loads + tables:
         copy.start()
 
-    for k in range(1, nd):
-        pl.semaphore_signal(bar, inc=1, device_id=along_dev(k), device_id_type=MESH)
-    for k in range(1, ng):
-        pl.semaphore_signal(bar, inc=1, device_id=along_grp(k), device_id_type=MESH)
+    for stage in range(STAGES):
+        for k in range(1, PEERS):
+            pl.semaphore_signal(bar, inc=1, device_id=peer(stage, k), device_id_type=MESH)
 
     kt[...] = jnp.zeros_like(kt)
     tk[...] = jnp.zeros_like(tk)
@@ -218,7 +224,7 @@
                 y = scr[pl.ds((s * 9 + b + 1) * GRP_CH, GRP_CH), :] * flag
                 white[s, b + 1, pl.ds(g * GRP_CH, GRP_CH), :] = y.astype(b16)
         if g == 0:
-            pl.semaphore_wait(bar, 4 + (nd - 1) + (ng - 1))
+            pl.semaphore_wait(bar, 4 + STAGES * (PEERS - 1))
             keep_copy(0).start()
             keep_copy(2).start()
         for s in range(EARLY):
@@ -294,21 +300,27 @@
     for copy in tables:
         copy.wait()
 
-    @pl.loop(0, SEG)
-    def _(s):
-        seg_copy(0, s).wait_recv()
-        seg_copy(1, s).start()
-
-        @pl.when(s < SEG - EARLY)
+    def last_dfts(s):
+        seg_copy(2, s).wait_recv()
+        own_dft(m2, s, 0, CH)
+        seg_copy(1, s).wait_recv()
+        window_dft(p2, s, (2 * CH, 4 * CH))
+
+    @pl.loop(0, SEG - 1 + LAG)
+    def _(step):
+        @pl.when(step < SEG)
         def _():
-            seg_copy(0, s + EARLY).start()
-
-        @pl.when(s > 0)
+            seg_copy(0, step).wait_recv()
+            seg_copy(1, step).start()
+
+        @pl.when(step < SEG - EARLY)
         def _():
-            seg_copy(2, s - 1).wait_recv()
-            own_dft(m2, s - 1, 0, CH)
-            seg_copy(1, s - 1).wait_recv()
-            window_dft(p2, s - 1, (2 * CH, 4 * CH))
+            seg_copy(0, step + EARLY).start()
+
+        @pl.when(step >= LAG)
+        def _():
+            first_dfts(step - LAG)
+            last_dfts(step - LAG)
 
             @pl.loop(0, CH // 8)
             def _(g):
@@ -317,7 +329,7 @@
                     accr[slot(g, j), :] = tr[j]
                     acci[slot(g, j), :] = ti[j]
 
-        first_dfts(s)
+    first_dfts(SEG - 1)
 
     keep_copy(1).wait_recv()
     keep_copy(2).wait_recv()
@@ -352,20 +364,26 @@
         y = jnp.dot(jnp.concatenate([hi, lo], axis=1), t_inv[...], preferred_element_type=f32)
         return y[:, :NLAG] + y[:, NLAG:]
 
-    def sum_copy(src, got, sem, k, to):
+    def sum_copy(stage, k):
         return pltpu.make_async_remote_copy(
-            src_ref=src,
-            dst_ref=got.at[k],
-            send_sem=sem.at[0, k],
-            recv_sem=sem.at[1, k],
-            device_id=to,
+            src_ref=got.at[stage, 0],
+            dst_ref=got.at[stage, k],
+            send_sem=qsem.at[0, stage, k],
+            recv_sem=qsem.at[1, stage, k],
+            device_id=peer(stage, k),
             device_id_type=MESH,
         )
 
-    seg_copy(2, SEG - 1).wait_recv()
-    own_dft(m2, SEG - 1, 0, CH)
-    seg_copy(1, SEG - 1).wait_recv()
-    window_dft(p2, SEG - 1, (2 * CH, 4 * CH))
+    def sum_start(stage):
+        for k in range(1, PEERS):
+            sum_copy(stage, k).start()
+
+    def sum_wait(stage):
+        for k in range(1, PEERS):
+            sum_copy(stage, k).wait_recv()
+        return jnp.sum(got[stage], axis=0)
+
+    last_dfts(SEG - 1)
 
     def finish(g, sums):
         tr, ti = pair_sums(g)
@@ -381,9 +399,9 @@
     zero = jnp.zeros((8, BLK), f32)
     sums = lax.fori_loop(0, CH // 8, finish, [zero] * (2 * NOFF))
     sums = [jnp.sum(t, axis=0, keepdims=True) for t in sums]
-    part[...] = lags(jnp.concatenate(sums[:NOFF], axis=0), jnp.concatenate(sums[NOFF:], axis=0))
-    for k in range(1, ng):
-        sum_copy(part, got_a, asem, k, along_grp(k)).start()
+    part = lags(jnp.concatenate(sums[:NOFF], axis=0), jnp.concatenate(sums[NOFF:], axis=0))
+    got[0, 0] = part
+    sum_start(0)
 
     for q in range(QUART):
         at = pl.ds(q * per * NOFF, per * NOFF)
@@ -392,12 +410,9 @@
         res_send[at, :] = corr.astype(b16)
         back_copy(q).start()
 
-    got_a[0] = part[...]
-    for k in range(1, ng):
-        sum_copy(part, got_a, asem, k, along_grp(k)).wait_recv()
-    got_b[0] = jnp.sum(got_a[...], axis=0)
-    for k in range(1, nd):
-        sum_copy(got_b.at[0], got_b, bsem, k, along_dev(k)).start()
+    for stage in range(1, STAGES):
+        got[stage, 0] = sum_wait(stage - 1)
+        sum_start(stage)
 
     for q in range(QUART):
         back_copy(q).wait_recv()
@@ -410,14 +425,10 @@
                 val = jnp.where(away(j, r0), theirs[h * 8 : h * 8 + 8], mine[h * 8 : h * 8 + 8])
                 out[pl.ds(r0 * NOFF + j, 8, stride=NOFF), :] = val
 
-    for k in range(1, nd):
-        sum_copy(got_b.at[0], got_b, bsem, k, along_dev(k)).wait_recv()
-    stack[...] = jnp.sum(got_b[...], axis=0) * (1.0 / math.sqrt(CH * nd * ng))
-
-    for k in range(1, ng):
-        sum_copy(part, got_a, asem, k, along_grp(k)).wait_send()
-    for k in range(1, nd):
-        sum_copy(got_b.at[0], got_b, bsem, k, along_dev(k)).wait_send()
+    stack[...] = sum_wait(STAGES - 1) * (1.0 / math.sqrt(CH * nd * ng))
+    for stage in range(STAGES):
+        for k in range(1, PEERS):
+            sum_copy(stage, k).wait_send()
     for q in range(QUART):
         back_copy(q).wait_send()
 
@@ -478,13 +489,10 @@
             vm((pairs, NLAG), f32),
             vm((pairs, NLAG), b16),
             vm((pairs, NLAG), b16),
-            vm((NOFF, NLAG), f32),
-            vm((ng, NOFF, NLAG), f32),
-            vm((nd, NOFF, NLAG), f32),
+            vm((STAGES, PEERS, NOFF, NLAG), f32),
             pltpu.SemaphoreType.DMA((4, SEG + 1)),
             pltpu.SemaphoreType.DMA((4, SEG + 1)),
-            pltpu.SemaphoreType.DMA((2, ng)),
-            pltpu.SemaphoreType.DMA((2, nd)),
+            pltpu.SemaphoreType.DMA((2, STAGES, PEERS)),
             pltpu.SemaphoreType.DMA((CH // GRP_CH + 5,)),
         ],
         compiler_params=pltpu.CompilerParams(

time: 75.1 us -> 67.2 us (0.89)
  Pallas kernels: 72 us -> 64.2 us
    pallas_call x1, Pallas kernels: 72 us -> 64.2 us  [local(): pl.pallas_call(functools.partial(kernel, shape), out_shape=(jax.ShapeDtyp...]
where the time goes in v4:
time: 67.2 us; the launch traced here: 67.1 us
  Pallas kernels  64.2 us (96%)
  local copies, waits for them, and re-layouts  2.27 us (3%)
    pallas_call x1, Pallas kernels, local(): pl.pallas_call(functools.partial(kernel, shape), out_shape=(jax.ShapeDtyp...  64.2 us
    unnamed x4, local copies, waits for them, and re-layouts  2.27 us

profile of v4, /device:TPU:1, one launch (start us, length us, event | category | flops | bytes accessed | tf_op | source)
XLA Modules:
  0.0 67.1 jit_solution(7185118675791099026)
XLA Ops:
  0.6 64.2 %whiten_correlate.1 = (f32[512,128]{1,0:T(8,128)}, f32[8,128]{1,0:T(8,128)}) custom-call(bf16[6,64,1024]{2,1,0:T(8,128)(2,1)} %bitcast.3, bf16[64,64]{1,0:T(8,128)(2,1)} %taps_hbm.1, s32[6,64]{1,0:T(8,128)} %bitcast.5, s32[8]{0:T(128)} %offs.1, bf16[256,256]{1,0:T(8,128)(2,1)} %constant.6.clone.own_hbm, bf16[512,256]{1,0:T(8,128)(2,1)} %constant.7.clone.win_hbm, ...), custom_call_target="tpu_custom_call" | custom-call | tf_op jit(solution)/shard_map/whiten_correlate/pallas_call | solution.py:454
  64.8 0.0 copy-start
  64.8 1.7 %copy.11 = f32[64,8,128]{2,1,0:T(8,128)} copy(f32[64,8,128]{2,1,0:T(8,128)} %bitcast.4) | data formatting | bytes 524288
  66.5 0.0 copy-done
  66.5 0.6 copy.12
Async XLA Ops:
  64.8 1.7 %copy-start = (f32[8,128]{1,0:T(8,128)S(1)}, f32[8,128]{1,0:T(8,128)}, u32[]{:S(2)}) copy-start(f32[8,128]{1,0:T(8,128)} %get-tuple-element.9) | copy-start | bytes 12292

commit v5 on v4

--- a/solution.py
+++ b/solution.py
@@ -24,8 +24,12 @@
 QUART = 4
 STAGES = 2
 EARLY = 3
-LAG = 2
+LAG = 3
 PEERS = 16
+FAR = (
+    sorted(range(1, 16), key=lambda k: -(min(k // 4, 4 - k // 4) + (k // 2) % 2 * 2 + k % 2)),
+    sorted(range(1, 16), key=lambda k: -min(k // 2, 8 - k // 2)),
+)
 MESH = pl.DeviceIdType.MESH
 
 
@@ -66,7 +70,7 @@
     own_hbm,
     win_hbm,
     inv_hbm,
-    out,
+    out_hbm,
     stack,
     ser,
     taps_in,
@@ -94,6 +98,7 @@
     accr,
     acci,
     scale,
+    out,
     res,
     res_send,
     res_recv,
@@ -243,7 +248,7 @@
     accr[...] = jnp.zeros_like(accr)
     acci[...] = jnp.zeros_like(acci)
 
-    def window_dft(src, s, bases):
+    def window_dft(src, s, turn, bases):
         nxt = jnp.where(row_lane < BLK // 2, 1.0, 0.0).astype(b16)
         prv = jnp.where(row_lane < BLK // 2, 0.0, 1.0).astype(b16)
         cur = src[s, pl.ds(1, NB)].reshape(ROWS, BLK)
@@ -252,15 +257,15 @@
         y = jnp.dot(x, t_win[...], preferred_element_type=f32)
         for b in range(NB):
             for base in bases:
-                yr[pl.ds(b * EXT + base, CH), :] = y[b * CH : (b + 1) * CH, :BLK]
-                yi[pl.ds(b * EXT + base, CH), :] = y[b * CH : (b + 1) * CH, BLK:]
-
-    def own_dft(src, s, start, base):
+                yr[turn, pl.ds(b * EXT + base, CH), :] = y[b * CH : (b + 1) * CH, :BLK]
+                yi[turn, pl.ds(b * EXT + base, CH), :] = y[b * CH : (b + 1) * CH, BLK:]
+
+    def own_dft(src, s, turn, start, base):
         w = src[s, pl.ds(start, NB)].reshape(ROWS, BLK)
         y = jnp.dot(jnp.concatenate([w, w], axis=1), t_own[...], preferred_element_type=f32)
         for b in range(NB):
-            xr[pl.ds(b * 2 * CH + base, CH), :] = y[b * CH : (b + 1) * CH, :BLK]
-            xi[pl.ds(b * 2 * CH + base, CH), :] = y[b * CH : (b + 1) * CH, BLK:]
+            xr[turn, pl.ds(b * 2 * CH + base, CH), :] = y[b * CH : (b + 1) * CH, :BLK]
+            xi[turn, pl.ds(b * 2 * CH + base, CH), :] = y[b * CH : (b + 1) * CH, BLK:]
 
     eight = lax.broadcasted_iota(jnp.int32, (8, BLK), 0)
     per = CH // QUART
@@ -272,39 +277,39 @@
         first = (g // (per // 8)) * (per * NOFF) + lax.rem(g, per // 8) * 8
         return pl.ds(pl.multiple_of(first + j * per, 8), 8)
 
-    def pair_sums(g):
+    def pair_sums(turn, g):
         r0 = pl.multiple_of(g * 8, 8)
         far = [away(j, r0) for j in range(NOFF)]
         tr = [accr[slot(g, j), :] for j in range(NOFF)]
         ti = [acci[slot(g, j), :] for j in range(NOFF)]
         for b in range(NB):
-            ar = xr[pl.ds(b * 2 * CH + r0, 8), :]
-            ai = xi[pl.ds(b * 2 * CH + r0, 8), :]
-            cr = xr[pl.ds(b * 2 * CH + CH + r0, 8), :]
-            ci = xi[pl.ds(b * 2 * CH + CH + r0, 8), :]
+            ar = xr[turn, pl.ds(b * 2 * CH + r0, 8), :]
+            ai = xi[turn, pl.ds(b * 2 * CH + r0, 8), :]
+            cr = xr[turn, pl.ds(b * 2 * CH + CH + r0, 8), :]
+            ci = xi[turn, pl.ds(b * 2 * CH + CH + r0, 8), :]
             for j in range(NOFF):
                 near = pl.ds(b * EXT + r0 + offs[j], 8)
-                br = yr[near, :]
-                bi = yi[near, :]
+                br = yr[turn, near, :]
+                bi = yi[turn, near, :]
                 lr = jnp.where(far[j], cr, ar)
                 li = jnp.where(far[j], ci, ai)
                 tr[j] = tr[j] + (lr * br + li * bi)
                 ti[j] = ti[j] + (lr * bi - li * br)
         return tr, ti
 
-    def first_dfts(s):
-        own_dft(white, s, 1, 0)
-        window_dft(white, s, (0,))
-        window_dft(p1, s, (CH, 3 * CH))
+    def first_dfts(s, turn):
+        own_dft(white, s, turn, 1, 0)
+        window_dft(white, s, turn, (0,))
+        window_dft(p1, s, turn, (CH, 3 * CH))
 
     for copy in tables:
         copy.wait()
 
-    def last_dfts(s):
+    def last_dfts(s, turn):
         seg_copy(2, s).wait_recv()
-        own_dft(m2, s, 0, CH)
+        own_dft(m2, s, turn, 0, CH)
         seg_copy(1, s).wait_recv()
-        window_dft(p2, s, (2 * CH, 4 * CH))
+        window_dft(p2, s, turn, (2 * CH, 4 * CH))
 
     @pl.loop(0, SEG - 1 + LAG)
     def _(step):
@@ -319,17 +324,19 @@
 
         @pl.when(step >= LAG)
         def _():
-            first_dfts(step - LAG)
-            last_dfts(step - LAG)
+            turn = lax.rem(step - LAG, LAG)
+            last_dfts(step - LAG, turn)
 
             @pl.loop(0, CH // 8)
             def _(g):
-                tr, ti = pair_sums(g)
+                tr, ti = pair_sums(turn, g)
                 for j in range(NOFF):
                     accr[slot(g, j), :] = tr[j]
                     acci[slot(g, j), :] = ti[j]
 
-    first_dfts(SEG - 1)
+        @pl.when(step < SEG)
+        def _():
+            first_dfts(step, lax.rem(step, LAG))
 
     keep_copy(1).wait_recv()
     keep_copy(2).wait_recv()
@@ -356,6 +363,10 @@
     def back_copy(q):
         rows = pl.ds(q * per * NOFF, per * NOFF)
         return remote(res_send.at[rows], res_recv.at[rows], 3, q, -2)
+
+    def out_copy(q):
+        rows = pl.ds(q * per * NOFF, per * NOFF)
+        return pltpu.make_async_copy(out.at[rows], out_hbm.at[rows], lsem.at[q])
 
     def lags(re, im):
         spec = jnp.concatenate([re, im], axis=1)
@@ -375,7 +386,7 @@
         )
 
     def sum_start(stage):
-        for k in range(1, PEERS):
+        for k in FAR[stage]:
             sum_copy(stage, k).start()
 
     def sum_wait(stage):
@@ -383,10 +394,11 @@
             sum_copy(stage, k).wait_recv()
         return jnp.sum(got[stage], axis=0)
 
-    last_dfts(SEG - 1)
+    turn = (SEG - 1) % LAG
+    last_dfts(SEG - 1, turn)
 
     def finish(g, sums):
-        tr, ti = pair_sums(g)
+        tr, ti = pair_sums(turn, g)
         new = []
         for j in range(NOFF):
             by = scale[slot(g, j), :]
@@ -424,12 +436,14 @@
                 r0 = q * per + h * 8
                 val = jnp.where(away(j, r0), theirs[h * 8 : h * 8 + 8], mine[h * 8 : h * 8 + 8])
                 out[pl.ds(r0 * NOFF + j, 8, stride=NOFF), :] = val
+        out_copy(q).start()
 
     stack[...] = sum_wait(STAGES - 1) * (1.0 / math.sqrt(CH * nd * ng))
     for stage in range(STAGES):
         for k in range(1, PEERS):
             sum_copy(stage, k).wait_send()
     for q in range(QUART):
+        out_copy(q).wait()
         back_copy(q).wait_send()
 
     @pl.loop(0, SEG)
@@ -458,7 +472,7 @@
             jax.ShapeDtypeStruct((NOFF, NLAG), f32),
         ),
         in_specs=[hbm, hbm, hbm, smem, hbm, hbm, hbm],
-        out_specs=(vmem, vmem),
+        out_specs=(hbm, vmem),
         scratch_shapes=[
             vm((SEG, CH, SAMP), b16),
             vm((CH, TAPS), b16),
@@ -479,13 +493,14 @@
             vm((SEG * 9 * GRP_CH, BLK), f32),
             vm((EXT, BLK), f32),
             vm((2 * CH, BLK), f32),
-            vm((NB * 2 * CH, BLK), f32),
-            vm((NB * 2 * CH, BLK), f32),
-            vm((NB * EXT, BLK), f32),
-            vm((NB * EXT, BLK), f32),
+            vm((LAG, NB * 2 * CH, BLK), f32),
+            vm((LAG, NB * 2 * CH, BLK), f32),
+            vm((LAG, NB * EXT, BLK), f32),
+            vm((LAG, NB * EXT, BLK), f32),
             vm((pairs, BLK), f32),
             vm((pairs, BLK), f32),
             vm((pairs, BLK), f32),
+            vm((pairs, NLAG), f32),
             vm((pairs, NLAG), f32),
             vm((pairs, NLAG), b16),
             vm((pairs, NLAG), b16),

time: 67.2 us -> 65.9 us (0.981)
  Pallas kernels: 64.2 us -> 62.8 us
    pallas_call x1, Pallas kernels: 64.2 us -> 62.8 us  [local(): pl.pallas_call(functools.partial(kernel, shape), out_shape=(jax.ShapeDtyp...]
where the time goes in v5:
time: 65.9 us; the launch traced here: 65.7 us
  Pallas kernels  62.8 us (95%)
  local copies, waits for them, and re-layouts  2.27 us (3%)
    pallas_call x1, Pallas kernels, local(): pl.pallas_call(functools.partial(kernel, shape), out_shape=(jax.ShapeDtyp...  62.8 us
    unnamed x4, local copies, waits for them, and re-layouts  2.27 us

profile of v5, /device:TPU:1, one launch (start us, length us, event | category | flops | bytes accessed | tf_op | source)
XLA Modules:
  0.0 65.7 jit_solution(6159682201107506203)
XLA Ops:
  0.6 62.8 %whiten_correlate.1 = (f32[512,128]{1,0:T(8,128)}, f32[8,128]{1,0:T(8,128)}) custom-call(bf16[6,64,1024]{2,1,0:T(8,128)(2,1)} %bitcast.3, bf16[64,64]{1,0:T(8,128)(2,1)} %taps_hbm.1, s32[6,64]{1,0:T(8,128)} %bitcast.5, s32[8]{0:T(128)} %offs.1, bf16[256,256]{1,0:T(8,128)(2,1)} %constant.6.clone.own_hbm, bf16[512,256]{1,0:T(8,128)(2,1)} %constant.7.clone.win_hbm, ...), custom_call_target="tpu_custom_call" | custom-call | tf_op jit(solution)/shard_map/whiten_correlate/pallas_call | solution.py:468
  63.5 0.0 copy-start
  63.5 1.7 %copy.11 = f32[64,8,128]{2,1,0:T(8,128)} copy(f32[64,8,128]{2,1,0:T(8,128)} %bitcast.4) | data formatting | bytes 524288
  65.1 0.0 copy-done
  65.1 0.6 copy.12
Async XLA Ops:
  63.5 1.7 %copy-start = (f32[8,128]{1,0:T(8,128)S(1)}, f32[8,128]{1,0:T(8,128)}, u32[]{:S(2)}) copy-start(f32[8,128]{1,0:T(8,128)} %get-tuple-element.9) | copy-start | bytes 12292

commit v6 on v5

--- a/solution.py
+++ b/solution.py
@@ -25,6 +25,7 @@
 STAGES = 2
 EARLY = 3
 LAG = 3
+PIECES = 4
 PEERS = 16
 FAR = (
     sorted(range(1, 16), key=lambda k: -(min(k // 4, 4 - k // 4) + (k // 2) % 2 * 2 + k % 2)),
@@ -453,6 +454,26 @@
 
     for line in range(3):
         keep_copy(line).wait_send()
+
+
+def hand_over(corr_in, stack_in, corr, stack, held, small, sem):
+    rows = CH * NOFF // PIECES
+    parts = [pl.ds(i * rows, rows) for i in range(PIECES)]
+    inward = [
+        pltpu.make_async_copy(corr_in.at[p], held.at[p], sem.at[0, i]) for i, p in enumerate(parts)
+    ]
+    inward.append(pltpu.make_async_copy(stack_in, small, sem.at[0, PIECES]))
+    outward = [
+        pltpu.make_async_copy(held.at[p], corr.at[p], sem.at[1, i]) for i, p in enumerate(parts)
+    ]
+    outward.append(pltpu.make_async_copy(small, stack, sem.at[1, PIECES]))
+    for copy in inward:
+        copy.start()
+    for arrived, leaving in zip(inward, outward):
+        arrived.wait()
+        leaving.start()
+    for copy in outward:
+        copy.wait()
 
 
 def local(shape, series, taps, keep, offsets):
@@ -515,6 +536,22 @@
         ),
         name="whiten_correlate",
     )(ser, taps, keep_rows, offsets, *dft_tables())
+    corr, stack = pl.pallas_call(
+        hand_over,
+        out_shape=(
+            jax.ShapeDtypeStruct((pairs, NLAG), f32),
+            jax.ShapeDtypeStruct((NOFF, NLAG), f32),
+        ),
+        in_specs=[hbm, hbm],
+        out_specs=(hbm, hbm),
+        scratch_shapes=[
+            vm((pairs, NLAG), f32),
+            vm((NOFF, NLAG), f32),
+            pltpu.SemaphoreType.DMA((2, PIECES + 1)),
+        ],
+        compiler_params=pltpu.CompilerParams(vmem_limit_bytes=60 << 20),
+        name="hand_over",
+    )(corr, stack)
     return corr.reshape(CH, NOFF, NLAG), stack
 
 

time: 65.9 us -> 65.3 us (level)
  local copies, waits for them, and re-layouts: 2.27 us -> 0 us
  Pallas kernels: 62.8 us -> 64.5 us
    unnamed x4 -> x0, local copies, waits for them, and re-layouts: 2.27 us -> none
    pallas_call x0 -> x1, Pallas kernels: none -> 1.65 us  [local(): pl.pallas_call(hand_over, out_shape=(jax.ShapeDtypeStruct((pairs, NLAG),...]
where the time goes in v6:
time: 65.3 us; the launch traced here: 65.1 us
  Pallas kernels  64.5 us (99%)
    pallas_call x1, Pallas kernels, local(): pl.pallas_call(functools.partial(kernel, shape), out_shape=(jax.ShapeDtyp...  62.8 us
    pallas_call x1, Pallas kernels, local(): pl.pallas_call(hand_over, out_shape=(jax.ShapeDtypeStruct((pairs, NLAG),...  1.65 us

profile of v6, /device:TPU:1, one launch (start us, length us, event | category | flops | bytes accessed | tf_op | source)
XLA Modules:
  0.0 65.1 jit_solution(8572394738485492164)
XLA Ops:
  0.6 62.8 %whiten_correlate.1 = (f32[512,128]{1,0:T(8,128)}, f32[8,128]{1,0:T(8,128)}) custom-call(bf16[6,64,1024]{2,1,0:T(8,128)(2,1)} %bitcast.3, bf16[64,64]{1,0:T(8,128)(2,1)} %taps_hbm.1, s32[6,64]{1,0:T(8,128)} %bitcast.4, s32[8]{0:T(128)} %offs.1, bf16[256,256]{1,0:T(8,128)(2,1)} %constant.6.clone.own_hbm, bf16[512,256]{1,0:T(8,128)(2,1)} %constant.7.clone.win_hbm, ...), custom_call_target="tpu_custom_call" | custom-call | tf_op jit(solution)/shard_map/whiten_correlate/pallas_call | solution.py:489
  63.5 1.7 %hand_over.1 = (f32[512,128]{1,0:T(8,128)}, f32[8,128]{1,0:T(8,128)}) custom-call(f32[512,128]{1,0:T(8,128)} %get-tuple-element.6.corr_in, f32[8,128]{1,0:T(8,128)} %get-tuple-element.7.stack_in), custom_call_target="tpu_custom_call" | custom-call | tf_op jit(solution)/shard_map/hand_over/pallas_call | solution.py:539

commit v7 on v6

--- a/solution.py
+++ b/solution.py
@@ -28,8 +28,8 @@
 PIECES = 4
 PEERS = 16
 FAR = (
+    sorted(range(1, 16), key=lambda k: -min(k // 2, 8 - k // 2)),
     sorted(range(1, 16), key=lambda k: -(min(k // 4, 4 - k // 4) + (k // 2) % 2 * 2 + k % 2)),
-    sorted(range(1, 16), key=lambda k: -min(k // 2, 8 - k // 2)),
 )
 MESH = pl.DeviceIdType.MESH
 
@@ -123,7 +123,7 @@
 
     def peer(stage, k):
         c, yy, xh, xl, zz = core, my_y, x_hi, x_lo, z
-        if stage == 0:
+        if stage == 1:
             yy = lax.rem(my_y + k // 4, 4)
             xh, xl = lax.rem(x_hi + k // 2 % 2, 2), lax.rem(x_lo + k % 2, 2)
         else:
@@ -439,7 +439,6 @@
                 out[pl.ds(r0 * NOFF + j, 8, stride=NOFF), :] = val
         out_copy(q).start()
 
-    stack[...] = sum_wait(STAGES - 1) * (1.0 / math.sqrt(CH * nd * ng))
     for stage in range(STAGES):
         for k in range(1, PEERS):
             sum_copy(stage, k).wait_send()
@@ -454,6 +453,7 @@
 
     for line in range(3):
         keep_copy(line).wait_send()
+    stack[...] = sum_wait(STAGES - 1) * (1.0 / math.sqrt(CH * nd * ng))
 
 
 def hand_over(corr_in, stack_in, corr, stack, held, small, sem):

time: 65.3 us -> 64.3 us (0.985)
  Pallas kernels: 64.5 us -> 63.4 us
    pallas_call x1, Pallas kernels: 62.8 us -> 61.8 us  [local(): pl.pallas_call(functools.partial(kernel, shape), out_shape=(jax.ShapeDtyp...]
where the time goes in v7:
time: 64.3 us; the launch traced here: 64.1 us
  Pallas kernels  63.4 us (99%)
    pallas_call x1, Pallas kernels, local(): pl.pallas_call(functools.partial(kernel, shape), out_shape=(jax.ShapeDtyp...  61.8 us
    pallas_call x1, Pallas kernels, local(): pl.pallas_call(hand_over, out_shape=(jax.ShapeDtypeStruct((pairs, NLAG),...  1.65 us

profile of v7, /device:TPU:1, one launch (start us, length us, event | category | flops | bytes accessed | tf_op | source)
XLA Modules:
  0.0 64.1 jit_solution(14739162358126158453)
XLA Ops:
  0.6 61.8 %whiten_correlate.1 = (f32[512,128]{1,0:T(8,128)}, f32[8,128]{1,0:T(8,128)}) custom-call(bf16[6,64,1024]{2,1,0:T(8,128)(2,1)} %bitcast.3, bf16[64,64]{1,0:T(8,128)(2,1)} %taps_hbm.1, s32[6,64]{1,0:T(8,128)} %bitcast.4, s32[8]{0:T(128)} %offs.1, bf16[256,256]{1,0:T(8,128)(2,1)} %constant.6.clone.own_hbm, bf16[512,256]{1,0:T(8,128)(2,1)} %constant.7.clone.win_hbm, ...), custom_call_target="tpu_custom_call" | custom-call | tf_op jit(solution)/shard_map/whiten_correlate/pallas_call | solution.py:489
  62.4 1.7 %hand_over.1 = (f32[512,128]{1,0:T(8,128)}, f32[8,128]{1,0:T(8,128)}) custom-call(f32[512,128]{1,0:T(8,128)} %get-tuple-element.6.corr_in, f32[8,128]{1,0:T(8,128)} %get-tuple-element.7.stack_in), custom_call_target="tpu_custom_call" | custom-call | tf_op jit(solution)/shard_map/hand_over/pallas_call | solution.py:539

commit v8 on v7

--- a/solution.py
+++ b/solution.py
@@ -130,10 +130,6 @@
             zz, c = lax.rem(z + k // 2, 8), lax.rem(core + k % 2, 2)
         return ((xh * 4 + yy) * 2 + c, xl * 8 + zz)
 
-    bar = pltpu.get_barrier_semaphore()
-    for k in (-2, -1, 1, 2):
-        pl.semaphore_signal(bar, inc=1, device_id=dev(k), device_id_type=MESH)
-
     groups = CH // GRP_CH
     small = [
         pltpu.make_async_copy(taps_hbm, taps_in, lsem.at[groups]),
@@ -153,6 +149,10 @@
     ]
     for copy in small + loads + tables:
         copy.start()
+
+    bar = pltpu.get_barrier_semaphore()
+    for k in (-2, -1, 1, 2):
+        pl.semaphore_signal(bar, inc=1, device_id=dev(k), device_id_type=MESH)
 
     for stage in range(STAGES):
         for k in range(1, PEERS):

time: 64.3 us -> 64.3 us (level)
  no operation moved by 1% of the time
where the time goes in v8:
time: 64.3 us; the launch traced here: 64.1 us
  Pallas kernels  63.4 us (99%)
    pallas_call x1, Pallas kernels, local(): pl.pallas_call(functools.partial(kernel, shape), out_shape=(jax.ShapeDtyp...  61.8 us
    pallas_call x1, Pallas kernels, local(): pl.pallas_call(hand_over, out_shape=(jax.ShapeDtypeStruct((pairs, NLAG),...  1.65 us

profile of v8, /device:TPU:1, one launch (start us, length us, event | category | flops | bytes accessed | tf_op | source)
XLA Modules:
  0.0 64.1 jit_solution(14812776818029427127)
XLA Ops:
  0.6 61.8 %whiten_correlate.1 = (f32[512,128]{1,0:T(8,128)}, f32[8,128]{1,0:T(8,128)}) custom-call(bf16[6,64,1024]{2,1,0:T(8,128)(2,1)} %bitcast.3, bf16[64,64]{1,0:T(8,128)(2,1)} %taps_hbm.1, s32[6,64]{1,0:T(8,128)} %bitcast.4, s32[8]{0:T(128)} %offs.1, bf16[256,256]{1,0:T(8,128)(2,1)} %constant.6.clone.own_hbm, bf16[512,256]{1,0:T(8,128)(2,1)} %constant.7.clone.win_hbm, ...), custom_call_target="tpu_custom_call" | custom-call | tf_op jit(solution)/shard_map/whiten_correlate/pallas_call | solution.py:489
  62.4 1.7 %hand_over.1 = (f32[512,128]{1,0:T(8,128)}, f32[8,128]{1,0:T(8,128)}) custom-call(f32[512,128]{1,0:T(8,128)} %get-tuple-element.6.corr_in, f32[8,128]{1,0:T(8,128)} %get-tuple-element.7.stack_in), custom_call_target="tpu_custom_call" | custom-call | tf_op jit(solution)/shard_map/hand_over/pallas_call | solution.py:539
